TPU v7x, 512 devices: a whole 4x4x16 slice. The times are simulated.
512 devices in a mesh: mode: 32 (over y, x, core), tm: 16 (over z).
Axes of the slice: x: 4, y: 4, z: 16, core: 2. Of those that a mesh axis runs over, the one named last changes fastest.
Arguments:
- field: float32 [2, 128, 65536], P(None, 'mode', 'tm'), may hold values from -1.8 to 1.8
- beta: float32 [3, 128], P(None, 'mode'), may hold values from -1 to 1
- quartets: int32 [4, 1024], replicated, may hold values from 0 to 127
- intersections: float32 [1024], replicated, may hold values from -0.12 to 0.12
Outputs:
- field_out: float32 [2, 128, 65536], P(None, 'mode', 'tm')
- errors: float32 [2, 128], P(None, 'mode')
All inputs are finite; a program needn't handle non-finite values.
Results may differ from a plain program's by a relative error of at most 0.0003.
Values sent between devices are 32-bit elements; how exact they have to be, the bound alone decides.
No kernel may reach another device: no remote copies, remote signals or barrier semaphores. Data moves between devices by JAX's collectives and lax.ppermute only.
A program may use at most 64 MiB of HBM per device.

v0:
```python
import functools
import math

import jax
import jax.numpy as jnp
import ml_dtypes
import numpy as np
from jax import lax
from jax.experimental import pallas as pl
from jax.experimental.pallas import tpu as pltpu
from jax.sharding import Mesh
from jax.sharding import PartitionSpec as P

STEPS = 2
LANES = 128
TIME = 65536
QUARTER = TIME // 4
TILE = 256
EPSILON = 1e-06
F32 = jnp.float32
BF16 = jnp.bfloat16


def two_parts(table):
    high = table.astype(ml_dtypes.bfloat16)
    low = (table - high.astype(np.float64)).astype(ml_dtypes.bfloat16)
    return (high, low)


def rows_table(table):
    high, low = two_parts(table)
    return np.concatenate([high, high, low], axis=1)


def lanes_table(table):
    high, low = two_parts(table)
    return np.concatenate([high, high, low], axis=0)


@functools.cache
def host_tables():
    index = np.arange(LANES)
    wave = np.exp(-2j * math.pi / LANES * (index[:, None] * index[None, :] % LANES))
    ahead = np.block([[wave.real, -wave.imag], [wave.imag, wave.real]])
    back = np.block([[wave.real, wave.imag], [-wave.imag, wave.real]])

    def row_order(place):
        return np.array([ri * LANES + p for p, ri in place])

    first_order = row_order(
        [
            (v2 * 32 + zb * 8 + rest, ri)
            for zb in range(4)
            for v2 in range(4)
            for ri in range(2)
            for rest in range(8)
        ]
    )
    later_order = row_order(
        [(v * 16 + w, ri) for w in range(16) for ri in range(2) for v in range(8)]
    )
    small = np.exp(-2j * math.pi / QUARTER * (index[:, None] * index[None, :] % QUARTER))

    def twist(place):
        angles = np.arange(4)[1:, None, None] * place[None]
        turned = np.exp(-2j * math.pi / TIME * (angles % TIME))
        return np.stack([turned.real, turned.imag], axis=1)

    rest = np.arange(8)[:, None] * LANES + index[None, :]
    entry = np.stack(
        [
            np.stack([twist(v2 * 4096 + zb * 1024 + rest) for v2 in range(4)])
            for zb in range(4)
        ]
    )
    v = np.arange(8)[:, None] * 2048 + index[None, :]
    middle = np.stack([twist(v + w * LANES) for w in range(16)])
    return {
        "first": rows_table(ahead[:, first_order]),
        "later": rows_table(ahead[:, later_order]),
        "ahead": lanes_table(ahead.T),
        "back": lanes_table(back.T),
        "leave": rows_table(back[later_order] / TIME),
        "small": np.stack([small.real, small.imag]).astype(np.float32),
        "entry": entry.astype(np.float32),
        "middle": middle.astype(np.float32),
    }


def split(array):
    high = array.astype(BF16)
    return (high, (array - high.astype(F32)).astype(BF16))


def dot(left, right):
    return jnp.dot(left, right, preferred_element_type=F32)


def from_left(table, array):
    high, low = split(array)
    return dot(table, jnp.concatenate([high, low, high], axis=0))


def from_right(array, table):
    high, low = split(array)
    return dot(jnp.concatenate([high, low, high], axis=1), table)


def enter_kernel(field_ref, out_ref):
    for ri in range(2):
        for tile in range(32):
            zb, rest = divmod(tile, 8)
            out_ref[pl.ds(zb * 16 + ri * 8 + rest, 4, stride=64), :] = field_ref[
                ri, :, tile * LANES : (tile + 1) * LANES
            ]


def radix_ahead(x):
    (r0, i0), (r1, i1), (r2, i2), (r3, i3) = x
    sr, si, dr, di = r0 + r2, i0 + i2, r0 - r2, i0 - i2
    tr, ti, ur, ui = r1 + r3, i1 + i3, r1 - r3, i1 - i3
    return [(sr + tr, si + ti), (dr + ui, di - ur), (sr - tr, si - ti), (dr - ui, di + ur)]


def radix_back(x):
    out = radix_ahead(x)
    return [out[0], out[3], out[2], out[1]]


def first_radix_kernel(zb_ref, x_ref, twist_ref, out_ref):
    for v2 in range(4):
        at = [a * 64 + v2 * 16 for a in range(4)]
        y = radix_ahead([(x_ref[b : b + 8, :], x_ref[b + 8 : b + 16, :]) for b in at])
        for f in range(4):
            re, im = y[f]
            if f:
                c, s = twist_ref[0, v2, f - 1, 0], twist_ref[0, v2, f - 1, 1]
                re, im = (re * c - im * s, re * s + im * c)
            out_ref[at[f] : at[f] + 8, :] = re
            out_ref[at[f] + 8 : at[f] + 16, :] = im


def ahead_kernel(w_ref, x_ref, twist_ref, out_ref):
    for low in range(4):
        y = radix_ahead(
            [
                tuple(x_ref[pl.ds(a * 64 + low * 2 + ri, 8, stride=8), :] for ri in range(2))
                for a in range(4)
            ]
        )
        for f in range(4):
            re, im = y[f]
            if f:
                c, s = twist_ref[0, f - 1, 0], twist_ref[0, f - 1, 1]
                re, im = (re * c - im * s, re * s + im * c)
            at = low * 64 + f * 16
            out_ref[at : at + 8, :] = re
            out_ref[at + 8 : at + 16, :] = im


def back_kernel(w_ref, x_ref, twist_ref, out_ref):
    for low in range(4):
        y = []
        for f in range(4):
            at = low * 64 + f * 16
            re, im = (x_ref[at : at + 8, :], x_ref[at + 8 : at + 16, :])
            if f:
                c, s = twist_ref[0, f - 1, 0], twist_ref[0, f - 1, 1]
                re, im = (re * c + im * s, im * c - re * s)
            y.append((re, im))
        for a, pair in enumerate(radix_back(y)):
            for ri in range(2):
                out_ref[pl.ds(a * 64 + low * 2 + ri, 8, stride=8), :] = pair[ri]


def cosine_and_sine(angle):
    scaled = angle * (2.0 / math.pi)
    turns = (scaled + jnp.where(scaled >= 0.0, 0.5, -0.5)).astype(jnp.int32)
    count = turns.astype(F32)
    x = angle - count * 1.5703125
    x = x - count * 4.837512969970703125e-4
    x = x - count * 7.5497899548918822e-8
    z = x * x
    sine = ((-1.9515295891e-4 * z + 8.3321608736e-3) * z - 1.6666654611e-1) * z * x + x
    cosine = (
        (2.443315711809948e-5 * z - 1.388731625493765e-3) * z + 4.166664568298827e-2
    ) * z * z - 0.5 * z + 1.0
    quarter = turns & 3
    odd = (quarter & 1) == 1
    c = jnp.where(odd, sine, cosine)
    s = jnp.where(odd, cosine, sine)
    c = jnp.where((quarter == 1) | (quarter == 2), -c, c)
    s = jnp.where(quarter >= 2, -s, s)
    return (c, s)


def spectral_kernel(
    place_ref, beta_ref, x_ref, into_ref, ahead_ref, back_ref, leave_ref, small_ref, out_ref
):
    low, f = (place_ref[0], place_ref[1])
    offset, slope, curve = (beta_ref[k, low] for k in range(3))
    shape = (LANES, LANES)
    wave = 4 * (
        lax.broadcasted_iota(jnp.int32, shape, 0)
        + LANES * lax.broadcasted_iota(jnp.int32, shape, 1)
    )
    wave = wave + f
    signed = jnp.where(wave < TIME // 2, wave, wave - TIME)
    frequency = signed.astype(F32) * (1.0 / (TIME / 2))
    angle = (
        math.pi * offset
        + 300.0 * slope * frequency
        + 3000.0 * curve * frequency * frequency
    )
    cosine, sine = cosine_and_sine(angle)
    small_re, small_im = (small_ref[0], small_ref[1])

    y = from_left(into_ref[...], x_ref[...])
    re, im = (y[:LANES], y[LANES:])
    re, im = (re * small_re - im * small_im, re * small_im + im * small_re)
    y = from_right(jnp.concatenate([re, im], axis=1), ahead_ref[...])
    re, im = (y[:, :LANES], y[:, LANES:])
    re, im = (re * cosine - im * sine, re * sine + im * cosine)
    y = from_right(jnp.concatenate([re, im], axis=1), back_ref[...])
    re, im = (y[:, :LANES], y[:, LANES:])
    re, im = (re * small_re + im * small_im, im * small_re - re * small_im)
    out_ref[...] = from_left(leave_ref[...], jnp.concatenate([re, im], axis=0))


def one_hot(row, count):
    ids = lax.broadcasted_iota(jnp.int32, (count, row.shape[1]), 0)
    return jnp.where(row == ids, 1.0, 0.0).astype(BF16)


def kerr_term(fields, quartets_ref, weights_ref):
    size = fields.shape[0] // 2
    parts = jnp.concatenate(split(fields), axis=1)
    total = None
    for start in range(0, quartets_ref.shape[1], TILE):
        here = slice(start, start + TILE)
        hot = [one_hot(quartets_ref[k : k + 1, here], fields.shape[1]) for k in range(4)]
        (lr, li), (mr, mi), (nr, ni) = (
            (y[:size], y[size:])
            for y in (dot(parts, jnp.concatenate([hot[k]] * 2, axis=0)) for k in (1, 2, 3))
        )
        weight = weights_ref[:, here]
        pr, pi = (lr * mr - li * mi, lr * mi + li * mr)
        pr, pi = (pr * weight, pi * weight)
        out_re, out_im = (pr * nr + pi * ni, pi * nr - pr * ni)
        terms = jnp.concatenate(split(jnp.concatenate([-out_im, out_re], axis=0)), axis=1)
        added = lax.dot_general(
            terms,
            jnp.concatenate([hot[0]] * 2, axis=1),
            (((1,), (1,)), ((), ())),
            preferred_element_type=F32,
        )
        total = added if total is None else total + added
    return total


def kerr_kernel(last, x_ref, quartets_ref, weights_ref, *refs):
    modes = x_ref.shape[0] // 2
    linear = jnp.concatenate(
        [x_ref[pl.ds(ri, modes, stride=2), :].T for ri in range(2)], axis=0
    )
    first = kerr_term(linear, quartets_ref, weights_ref)
    second = kerr_term(linear + first, quartets_ref, weights_ref)
    updated = linear + 0.5 * (first + second)
    estimate = 0.5 * (second - first)
    sums = [jnp.sum(y * y, axis=0, keepdims=True) for y in (estimate, updated)]
    if not last:
        out_ref, sums_ref = refs
        for ri in range(2):
            out_ref[pl.ds(ri, modes, stride=2), :] = updated[ri * LANES : (ri + 1) * LANES].T
        sums_ref[0:1, :] = sums[0]
        sums_ref[1:2, :] = sums[1]
        return
    before_ref, out_ref, held_ref = refs
    for ri in range(2):
        held_ref[pl.ds(ri, modes, stride=2), :] = updated[ri * LANES : (ri + 1) * LANES].T
    norms = jnp.concatenate([before_ref[0:2, :], *sums], axis=0)
    for group in range(modes // 4):
        out_ref[group * 12 : group * 12 + 8, :] = held_ref[group * 8 : group * 8 + 8, :]
        out_ref[group * 12 + 8 : group * 12 + 12, :] = norms


def regroup_kernel(group_ref, x_ref, out_ref):
    norms = x_ref[8:12, :]
    for source in range(1, 32):
        norms = norms + x_ref[source * 12 + 8 : source * 12 + 12, :]
    norms = pltpu.roll(norms, (LANES - 4 * group_ref[0]) % LANES, 1)
    lane = lax.broadcasted_iota(jnp.int32, (1, LANES), 1)
    own = jnp.where(lane < 4, norms[0:1, :], 0.0)
    for k in range(1, 4):
        moved = pltpu.roll(norms[k : k + 1, :], 4 * k, 1)
        own = jnp.where((lane >= 4 * k) & (lane < 4 * k + 4), moved, own)
    for target in range(16):
        for half in range(2):
            source = target * 2 + half
            at = target * 17 + half * 8
            out_ref[at : at + 8, :] = x_ref[source * 12 : source * 12 + 8, :]
        out_ref[target * 17 + 16 : target * 17 + 17, :] = own


def leave_kernel(x_ref, field_ref, errors_ref):
    norms = x_ref[16:17, :]
    for source in range(1, 16):
        norms = norms + x_ref[source * 17 + 16 : source * 17 + 17, :]
    size = pltpu.roll(norms, LANES - 4, 1)
    ratio = jnp.sqrt(norms / (size + EPSILON))
    errors_ref[0:1, :] = ratio[:, 0:4]
    errors_ref[1:2, :] = ratio[:, 8:12]
    for source in range(16):
        for half in range(2):
            tile = half * 16 + source
            for ri in range(2):
                field_ref[ri, :, tile * LANES : (tile + 1) * LANES] = x_ref[
                    pl.ds(source * 17 + half * 8 + ri, 4, stride=2), :
                ]


def rows_of(count):
    return jax.ShapeDtypeStruct((count, LANES), F32)


def picked(kernel, index, array, table, tail):
    zeros = (0,) * len(tail)
    return pl.pallas_call(
        kernel,
        out_shape=rows_of(array.shape[0]),
        grid_spec=pltpu.PrefetchScalarGridSpec(
            num_scalar_prefetch=1,
            grid=(1,),
            in_specs=[
                pl.BlockSpec(array.shape, lambda i, at: (0, 0)),
                pl.BlockSpec((1, *tail), lambda i, at: (at[0], *zeros)),
            ],
            out_specs=pl.BlockSpec(array.shape, lambda i, at: (0, 0)),
        ),
    )(index, array, table)


def exchange(array, axes, peers):
    tiles = array.reshape(peers, array.shape[0] // peers, LANES)
    return lax.all_to_all(tiles, axes, 0, 0, tiled=True).reshape(array.shape)


def shards(field, beta, quartets, intersections):
    tables = {name: jnp.asarray(value) for name, value in host_tables().items()}
    group = lax.axis_index("mode").astype(jnp.int32)[None]
    th, tl = (lax.axis_index("th"), lax.axis_index("tl"))
    place = jnp.stack([th, tl]).astype(jnp.int32)
    low_place = tl.astype(jnp.int32)[None]
    whole_place = (th * 4 + tl).astype(jnp.int32)[None]
    weights = intersections.reshape(1, -1)
    along, across = (("th", "tl"), "mode")
    vmem = pl.BlockSpec(memory_space=pltpu.VMEM)
    smem = pl.BlockSpec(memory_space=pltpu.SMEM)
    limit = pltpu.CompilerParams(vmem_limit_bytes=48 * 1024 * 1024)

    def spectral(state, into):
        return pl.pallas_call(
            spectral_kernel,
            out_shape=rows_of(256),
            in_specs=[smem, smem] + [vmem] * 6,
            out_specs=vmem,
            compiler_params=limit,
        )(place, beta, state, into, tables["ahead"], tables["back"], tables["leave"], tables["small"])

    state = pl.pallas_call(
        enter_kernel, out_shape=rows_of(256), in_specs=[vmem], out_specs=vmem
    )(field)
    state = exchange(state, along, 16)
    state = picked(first_radix_kernel, low_place, state, tables["entry"], (4, 3, 2, 8, LANES))
    state = exchange(state, "tl", 4)
    norms = []
    for step in range(STEPS):
        last = step == STEPS - 1
        state = spectral(state, tables["later" if step else "first"])
        state = exchange(state, along, 16)
        state = picked(back_kernel, whole_place, state, tables["middle"], (3, 2, 8, LANES))
        state = exchange(state, across, 32)
        out = pl.pallas_call(
            functools.partial(kerr_kernel, last),
            out_shape=rows_of(384) if last else (rows_of(256), rows_of(8)),
            in_specs=[vmem] * (3 + len(norms)),
            out_specs=vmem if last else (vmem, vmem),
            scratch_shapes=[pltpu.VMEM((256, LANES), F32)] if last else [],
            compiler_params=limit,
        )(state, quartets, weights, *norms)
        if last:
            state = exchange(out, across, 32)
            break
        state, norm = out
        norms.append(norm)
        state = exchange(state, across, 32)
        state = picked(ahead_kernel, whole_place, state, tables["middle"], (3, 2, 8, LANES))
        state = exchange(state, along, 16)
    state = pl.pallas_call(
        regroup_kernel, out_shape=rows_of(272), in_specs=[smem, vmem], out_specs=vmem
    )(group, state)
    state = exchange(state, along, 16)
    return pl.pallas_call(
        leave_kernel,
        out_shape=(
            jax.ShapeDtypeStruct(field.shape, F32),
            jax.ShapeDtypeStruct((STEPS, field.shape[1]), F32),
        ),
        in_specs=[vmem],
        out_specs=(vmem, vmem),
    )(state)


def solution(mesh):
    finer = Mesh(mesh.devices.reshape(-1, 4, 4), ("mode", "th", "tl"))
    times = ("th", "tl")
    return jax.shard_map(
        shards,
        mesh=finer,
        in_specs=(P(None, "mode", times), P(None, "mode"), P(), P()),
        out_specs=(P(None, "mode", times), P(None, "mode")),
        check_vma=False,
    )
```

profile of v0, /device:TPU:32, one launch (start us, length us, event | category | flops | bytes accessed | tf_op | source)
XLA Modules:
  0.0 192.0 jit_solution(3724824119152321130)
XLA Ops:
  0.6 1.7 shard_map.131
  2.3 15.3 %all-to-all-start = ((f32[16,16,128]{2,1,0:T(8,128)}), f32[16,16,128]{2,1,0:T(8,128)S(1)}, u32[]{:S(2)}, u32[]{:S(2)}) async-start(f32[16,16,128]{2,1,0:T(8,128)} %bitcast.29), calls=%async_computation | async-start | bytes 262144 | tf_op jit(solution)/shard_map/all_to_all | solution.py:345
  17.7 14.2 %all-to-all-done = f32[16,16,128]{2,1,0:T(8,128)S(1)} async-done(((f32[16,16,128]{2,1,0:T(8,128)}), f32[16,16,128]{2,1,0:T(8,128)S(1)}, u32[]{:S(2)}, u32[]{:S(2)}) %all-to-all-start) | async-done | bytes 131104 | tf_op jit(solution)/shard_map/all_to_all | solution.py:345
  32.5 1.7 shard_map.132
  34.3 3.9 %all-to-all-start.1 = ((f32[4,64,128]{2,1,0:T(8,128)}), f32[4,64,128]{2,1,0:T(8,128)S(1)}, u32[]{:S(2)}, u32[]{:S(2)}) async-start(f32[4,64,128]{2,1,0:T(8,128)} %bitcast.32), calls=%async_computation.1 | async-start | bytes 262144 | tf_op jit(solution)/shard_map/all_to_all | solution.py:345
  38.2 5.1 %all-to-all-done.1 = f32[4,64,128]{2,1,0:T(8,128)S(1)} async-done(((f32[4,64,128]{2,1,0:T(8,128)}), f32[4,64,128]{2,1,0:T(8,128)S(1)}, u32[]{:S(2)}, u32[]{:S(2)}) %all-to-all-start.1) | async-done | bytes 131104 | tf_op jit(solution)/shard_map/all_to_all | solution.py:345
  44.3 2.2 %shard_map.133 = f32[256,128]{1,0:T(8,128)} custom-call(s32[2]{0:T(128)S(1)} %pad_add_fusion.place_ref, f32[3,4]{1,0:T(4,128)S(1)} %copy-done.8, f32[256,128]{1,0:T(8,128)S(1)} %bitcast.21, bf16[256,768]{1,0:T(8,128)(2,1)S(1)} %copy-done.5, bf16[768,256]{1,0:T(8,128)(2,1)S(1)} %copy-done.2, bf16[768,256]{1,0:T(8,128)(2,1)S(1)} %copy-done.1, ...), custom_call_target="tpu_custom_call" | custom-call | tf_op jit(solution)/shard_map/pallas_call | solution.py:362
  46.5 5.6 %all-to-all-start.2 = ((f32[16,16,128]{2,1,0:T(8,128)}), f32[16,16,128]{2,1,0:T(8,128)S(1)}, u32[]{:S(2)}, u32[]{:S(2)}) async-start(f32[16,16,128]{2,1,0:T(8,128)} %bitcast.8), calls=%async_computation.2 | async-start | bytes 262144 | tf_op jit(solution)/shard_map/all_to_all | solution.py:345
  52.1 12.7 %all-to-all-done.2 = f32[16,16,128]{2,1,0:T(8,128)S(1)} async-done(((f32[16,16,128]{2,1,0:T(8,128)}), f32[16,16,128]{2,1,0:T(8,128)S(1)}, u32[]{:S(2)}, u32[]{:S(2)}) %all-to-all-start.2) | async-done | bytes 131104 | tf_op jit(solution)/shard_map/all_to_all | solution.py:345
  65.5 1.6 shard_map.134
  67.1 15.3 %all_to_all.50 = f32[32,8,128]{2,1,0:T(8,128)S(1)} all-to-all(f32[32,8,128]{2,1,0:T(8,128)} %bitcast.35), channel_id=1, replica_groups=mesh['mode'=32,'th'=4,'tl'=4] {'mode'}, dimensions={0} | all-to-all | bytes 262144 | tf_op jit(solution)/shard_map/all_to_all | solution.py:345
  82.4 2.3 %shard_map.135 = (f32[256,128]{1,0:T(8,128)S(1)}, f32[8,128]{1,0:T(8,128)S(1)}) custom-call(f32[256,128]{1,0:T(8,128)S(1)} %bitcast.24, s32[4,1024]{1,0:T(4,128)S(1)} %copy-done.6, f32[1,1024]{1,0:T(1,128)S(1)} %bitcast.27), custom_call_target="tpu_custom_call" | custom-call | tf_op jit(solution)/shard_map/pallas_call | solution.py:383
  84.7 11.5 %all_to_all.51 = f32[32,8,128]{2,1,0:T(8,128)} all-to-all(f32[32,8,128]{2,1,0:T(8,128)S(1)} %bitcast.26), channel_id=1, replica_groups=mesh['mode'=32,'th'=4,'tl'=4] {'mode'}, dimensions={0} | all-to-all | bytes 262144 | tf_op jit(solution)/shard_map/all_to_all | solution.py:345
  96.2 1.6 shard_map.136
  97.8 18.3 %all_to_all.52 = f32[16,16,128]{2,1,0:T(8,128)S(1)} all-to-all(f32[16,16,128]{2,1,0:T(8,128)} %bitcast.37), channel_id=1, replica_groups=mesh['mode'=32,'th'=4,'tl'=4] {'th','tl'}, dimensions={0} | all-to-all | bytes 262144 | tf_op jit(solution)/shard_map/all_to_all | solution.py:345
  117.6 19.3 %all_to_all.53 = f32[16,16,128]{2,1,0:T(8,128)} all-to-all(f32[16,16,128]{2,1,0:T(8,128)S(1)} %bitcast.23), channel_id=1, replica_groups=mesh['mode'=32,'th'=4,'tl'=4] {'th','tl'}, dimensions={0} | all-to-all | bytes 262144 | tf_op jit(solution)/shard_map/all_to_all | solution.py:345
  136.9 1.6 shard_map.138
  138.5 11.6 %all_to_all.54 = f32[32,8,128]{2,1,0:T(8,128)S(1)} all-to-all(f32[32,8,128]{2,1,0:T(8,128)} %bitcast.34), channel_id=1, replica_groups=mesh['mode'=32,'th'=4,'tl'=4] {'mode'}, dimensions={0} | all-to-all | bytes 262144 | tf_op jit(solution)/shard_map/all_to_all | solution.py:345
  150.1 2.4 %shard_map.139 = f32[384,128]{1,0:T(8,128)S(1)} custom-call(f32[256,128]{1,0:T(8,128)S(1)} %bitcast.25, s32[4,1024]{1,0:T(4,128)S(1)} %copy-done.6, f32[1,1024]{1,0:T(1,128)S(1)} %bitcast.28, f32[8,128]{1,0:T(8,128)S(1)} %get-tuple-element.5.refs_0_), custom_call_target="tpu_custom_call" | custom-call | tf_op jit(solution)/shard_map/pallas_call | solution.py:383
  153.2 3.9 %all-to-all-start.8 = ((f32[32,12,128]{2,1,0:T(8,128)}), f32[32,12,128]{2,1,0:T(8,128)S(1)}, u32[]{:S(2)}, u32[]{:S(2)}) async-start(f32[32,12,128]{2,1,0:T(8,128)} %reshape.84), calls=%async_computation.8 | async-start | bytes 524288 | tf_op jit(solution)/shard_map/all_to_all | solution.py:345
  157.1 8.9 %all-to-all-done.8 = f32[32,12,128]{2,1,0:T(8,128)S(1)} async-done(((f32[32,12,128]{2,1,0:T(8,128)}), f32[32,12,128]{2,1,0:T(8,128)S(1)}, u32[]{:S(2)}, u32[]{:S(2)}) %all-to-all-start.8) | async-done | bytes 196640 | tf_op jit(solution)/shard_map/all_to_all | solution.py:345
  166.7 1.8 shard_map.140
  169.3 20.4 %all_to_all.55 = f32[16,17,128]{2,1,0:T(8,128)S(1)} all-to-all(f32[16,17,128]{2,1,0:T(8,128)S(1)} %reshape.86), channel_id=1, replica_groups=mesh['mode'=32,'th'=4,'tl'=4] {'th','tl'}, dimensions={0} | all-to-all | bytes 278528 | tf_op jit(solution)/shard_map/all_to_all | solution.py:345
  190.4 1.7 shard_map.141
  (28 shorter events, 6.9 us)
Async XLA Ops:
  0.6 42.7 %copy-start.3 = (f32[2,128,128]{2,1,0:T(8,128)S(1)}, f32[2,128,128]{2,1,0:T(8,128)}, u32[]{:S(2)}) copy-start(f32[2,128,128]{2,1,0:T(8,128)} %constant.36.clone.small_ref) | copy-start | bytes 393220
  2.3 41.0 %copy-start.2 = (bf16[768,256]{1,0:T(8,128)(2,1)S(1)}, bf16[768,256]{1,0:T(8,128)(2,1)}, u32[]{:S(2)}) copy-start(bf16[768,256]{1,0:T(8,128)(2,1)} %constant.33.clone.ahead_ref) | copy-start | bytes 1179652
  2.3 29.6 %all-to-all-start = ((f32[16,16,128]{2,1,0:T(8,128)}), f32[16,16,128]{2,1,0:T(8,128)S(1)}, u32[]{:S(2)}, u32[]{:S(2)}) async-start(f32[16,16,128]{2,1,0:T(8,128)} %bitcast.29), calls=%async_computation | async-start | bytes 262144 | tf_op jit(solution)/shard_map/all_to_all | solution.py:345
  31.9 0.7 copy-start.10
  32.5 10.7 %copy-start = (bf16[256,768]{1,0:T(8,128)(2,1)S(1)}, bf16[256,768]{1,0:T(8,128)(2,1)}, u32[]{:S(2)}) copy-start(bf16[256,768]{1,0:T(8,128)(2,1)} %constant.35.clone.leave_ref) | copy-start | bytes 1179652
  32.5 10.7 %copy-start.1 = (bf16[768,256]{1,0:T(8,128)(2,1)S(1)}, bf16[768,256]{1,0:T(8,128)(2,1)}, u32[]{:S(2)}) copy-start(bf16[768,256]{1,0:T(8,128)(2,1)} %constant.34.clone.back_ref) | copy-start | bytes 1179652
  34.3 9.0 %all-to-all-start.1 = ((f32[4,64,128]{2,1,0:T(8,128)}), f32[4,64,128]{2,1,0:T(8,128)S(1)}, u32[]{:S(2)}, u32[]{:S(2)}) async-start(f32[4,64,128]{2,1,0:T(8,128)} %bitcast.32), calls=%async_computation.1 | async-start | bytes 262144 | tf_op jit(solution)/shard_map/all_to_all | solution.py:345
  38.1 5.2 %copy-start.8 = (f32[3,4]{1,0:T(4,128)S(1)}, f32[3,4]{1,0:T(4,128)}, u32[]{:S(2)}) copy-start(f32[3,4]{1,0:T(4,128)} %beta_ref.3) | copy-start | bytes 148
  43.3 1.0 copy-start.5
  46.5 18.4 %all-to-all-start.2 = ((f32[16,16,128]{2,1,0:T(8,128)}), f32[16,16,128]{2,1,0:T(8,128)S(1)}, u32[]{:S(2)}, u32[]{:S(2)}) async-start(f32[16,16,128]{2,1,0:T(8,128)} %bitcast.8), calls=%async_computation.2 | async-start | bytes 262144 | tf_op jit(solution)/shard_map/all_to_all | solution.py:345
  64.9 0.7 copy-start.9
  67.1 15.3 %copy-start.6 = (s32[4,1024]{1,0:T(4,128)S(1)}, s32[4,1024]{1,0:T(4,128)}, u32[]{:S(2)}) copy-start(s32[4,1024]{1,0:T(4,128)} %quartets_ref.3) | copy-start | bytes 49156
  67.1 15.3 %copy-start.7 = (f32[1024]{0:T(1024)S(1)}, f32[1024]{0:T(1024)}, u32[]{:S(2)}) copy-start(f32[1024]{0:T(1024)} %param.15) | copy-start | bytes 12292
  96.2 19.9 %copy-start.4 = (bf16[256,768]{1,0:T(8,128)(2,1)S(1)}, bf16[256,768]{1,0:T(8,128)(2,1)}, u32[]{:S(2)}) copy-start(bf16[256,768]{1,0:T(8,128)(2,1)} %constant.32.clone.into_ref) | copy-start | bytes 1179652
  153.2 12.8 %all-to-all-start.8 = ((f32[32,12,128]{2,1,0:T(8,128)}), f32[32,12,128]{2,1,0:T(8,128)S(1)}, u32[]{:S(2)}, u32[]{:S(2)}) async-start(f32[32,12,128]{2,1,0:T(8,128)} %reshape.84), calls=%async_computation.8 | async-start | bytes 524288 | tf_op jit(solution)/shard_map/all_to_all | solution.py:345
where the time goes:
time: 193 us; the launch traced here: 192 us
  blocking collectives  96.3 us (50%)
  waiting for transfers between devices  40.9 us (21%)
  starting transfers between devices  28.7 us (15%)
  Pallas kernels  20 us (10%)
  local copies, waits for them, and re-layouts  5.32 us (3%)
    all_to_all x6, blocking collectives, exchange(): return lax.all_to_all(tiles, axes, 0, 0, tiled=True).reshape(array.shape)  96.3 us
    all_to_all x4, waiting for transfers between devices, exchange(): return lax.all_to_all(tiles, axes, 0, 0, tiled=True).reshape(array.shape)  40.9 us
    all_to_all x4, starting transfers between devices, exchange(): return lax.all_to_all(tiles, axes, 0, 0, tiled=True).reshape(array.shape)  28.7 us
    pallas_call x4, Pallas kernels, picked(): pl.pallas_call(kernel, out_shape=rows_of(array.shape[0]), grid_spec=pltpu...  6.52 us
    pallas_call x2, Pallas kernels, shards(): pl.pallas_call(functools.partial(kerr_kernel, last), out_shape=rows_of(38...  4.69 us
  transfers between devices with their start and end apart: 4, of which 4 were waited for; matrix products, arithmetic and copies ran while one was open for 0% of the time, Pallas kernels for 0%

commit v1 on v0

--- a/solution.py
+++ b/solution.py
@@ -24,17 +24,7 @@
 def two_parts(table):
     high = table.astype(ml_dtypes.bfloat16)
     low = (table - high.astype(np.float64)).astype(ml_dtypes.bfloat16)
-    return (high, low)
-
-
-def rows_table(table):
-    high, low = two_parts(table)
-    return np.concatenate([high, high, low], axis=1)
-
-
-def lanes_table(table):
-    high, low = two_parts(table)
-    return np.concatenate([high, high, low], axis=0)
+    return np.stack([high, low])
 
 
 @functools.cache
@@ -47,16 +37,7 @@
     def row_order(place):
         return np.array([ri * LANES + p for p, ri in place])
 
-    first_order = row_order(
-        [
-            (v2 * 32 + zb * 8 + rest, ri)
-            for zb in range(4)
-            for v2 in range(4)
-            for ri in range(2)
-            for rest in range(8)
-        ]
-    )
-    later_order = row_order(
+    tile_order = row_order(
         [(v * 16 + w, ri) for w in range(16) for ri in range(2) for v in range(8)]
     )
     small = np.exp(-2j * math.pi / QUARTER * (index[:, None] * index[None, :] % QUARTER))
@@ -66,21 +47,20 @@
         turned = np.exp(-2j * math.pi / TIME * (angles % TIME))
         return np.stack([turned.real, turned.imag], axis=1)
 
-    rest = np.arange(8)[:, None] * LANES + index[None, :]
+    rest = np.array([v0 * 2048 + w * LANES for v0 in range(2) for w in range(4)])
+    rest = rest[:, None] + index[None, :]
     entry = np.stack(
-        [
-            np.stack([twist(v2 * 4096 + zb * 1024 + rest) for v2 in range(4)])
-            for zb in range(4)
-        ]
+        [np.stack([twist(v2 * 4096 + zb * 512 + rest) for v2 in range(4)]) for zb in range(4)]
     )
     v = np.arange(8)[:, None] * 2048 + index[None, :]
     middle = np.stack([twist(v + w * LANES) for w in range(16)])
     return {
-        "first": rows_table(ahead[:, first_order]),
-        "later": rows_table(ahead[:, later_order]),
-        "ahead": lanes_table(ahead.T),
-        "back": lanes_table(back.T),
-        "leave": rows_table(back[later_order] / TIME),
+        "waves": np.stack(
+            [
+                two_parts(table)
+                for table in (ahead[:, tile_order], ahead.T, back.T, back[tile_order] / TIME)
+            ]
+        ),
         "small": np.stack([small.real, small.imag]).astype(np.float32),
         "entry": entry.astype(np.float32),
         "middle": middle.astype(np.float32),
@@ -96,20 +76,24 @@
     return jnp.dot(left, right, preferred_element_type=F32)
 
 
-def from_left(table, array):
+def from_left(waves_ref, which, array):
     high, low = split(array)
-    return dot(table, jnp.concatenate([high, low, high], axis=0))
-
-
-def from_right(array, table):
+    return dot(waves_ref[which, 0], high) + (
+        dot(waves_ref[which, 0], low) + dot(waves_ref[which, 1], high)
+    )
+
+
+def from_right(array, waves_ref, which):
     high, low = split(array)
-    return dot(jnp.concatenate([high, low, high], axis=1), table)
+    return dot(high, waves_ref[which, 0]) + (
+        dot(low, waves_ref[which, 0]) + dot(high, waves_ref[which, 1])
+    )
 
 
 def enter_kernel(field_ref, out_ref):
     for ri in range(2):
         for tile in range(32):
-            zb, rest = divmod(tile, 8)
+            zb, rest = (tile // 4 % 4, tile // 16 * 4 + tile % 4)
             out_ref[pl.ds(zb * 16 + ri * 8 + rest, 4, stride=64), :] = field_ref[
                 ri, :, tile * LANES : (tile + 1) * LANES
             ]
@@ -127,20 +111,22 @@
     return [out[0], out[3], out[2], out[1]]
 
 
-def first_radix_kernel(zb_ref, x_ref, twist_ref, out_ref):
+def first_radix_kernel(x_ref, twist_ref, out_ref):
     for v2 in range(4):
         at = [a * 64 + v2 * 16 for a in range(4)]
         y = radix_ahead([(x_ref[b : b + 8, :], x_ref[b + 8 : b + 16, :]) for b in at])
         for f in range(4):
             re, im = y[f]
             if f:
-                c, s = twist_ref[0, v2, f - 1, 0], twist_ref[0, v2, f - 1, 1]
+                c, s = twist_ref[v2, f - 1, 0], twist_ref[v2, f - 1, 1]
                 re, im = (re * c - im * s, re * s + im * c)
-            out_ref[at[f] : at[f] + 8, :] = re
-            out_ref[at[f] + 8 : at[f] + 16, :] = im
-
-
-def ahead_kernel(w_ref, x_ref, twist_ref, out_ref):
+            for ri, part in enumerate((re, im)):
+                for v0 in range(2):
+                    first = f * 64 + ri * 8 + v2 * 2 + v0
+                    out_ref[pl.ds(first, 4, stride=16), :] = part[v0 * 4 : v0 * 4 + 4]
+
+
+def ahead_kernel(x_ref, twist_ref, out_ref):
     for low in range(4):
         y = radix_ahead(
             [
@@ -151,21 +137,21 @@
         for f in range(4):
             re, im = y[f]
             if f:
-                c, s = twist_ref[0, f - 1, 0], twist_ref[0, f - 1, 1]
+                c, s = twist_ref[f - 1, 0], twist_ref[f - 1, 1]
                 re, im = (re * c - im * s, re * s + im * c)
             at = low * 64 + f * 16
             out_ref[at : at + 8, :] = re
             out_ref[at + 8 : at + 16, :] = im
 
 
-def back_kernel(w_ref, x_ref, twist_ref, out_ref):
+def back_kernel(x_ref, twist_ref, out_ref):
     for low in range(4):
         y = []
         for f in range(4):
             at = low * 64 + f * 16
             re, im = (x_ref[at : at + 8, :], x_ref[at + 8 : at + 16, :])
             if f:
-                c, s = twist_ref[0, f - 1, 0], twist_ref[0, f - 1, 1]
+                c, s = twist_ref[f - 1, 0], twist_ref[f - 1, 1]
                 re, im = (re * c + im * s, im * c - re * s)
             y.append((re, im))
         for a, pair in enumerate(radix_back(y)):
@@ -195,7 +181,7 @@
 
 
 def spectral_kernel(
-    place_ref, beta_ref, x_ref, into_ref, ahead_ref, back_ref, leave_ref, small_ref, out_ref
+    place_ref, beta_ref, x_ref, waves_ref, small_ref, out_ref
 ):
     low, f = (place_ref[0], place_ref[1])
     offset, slope, curve = (beta_ref[k, low] for k in range(3))
@@ -215,16 +201,16 @@
     cosine, sine = cosine_and_sine(angle)
     small_re, small_im = (small_ref[0], small_ref[1])
 
-    y = from_left(into_ref[...], x_ref[...])
+    y = from_left(waves_ref, 0, x_ref[...])
     re, im = (y[:LANES], y[LANES:])
     re, im = (re * small_re - im * small_im, re * small_im + im * small_re)
-    y = from_right(jnp.concatenate([re, im], axis=1), ahead_ref[...])
+    y = from_right(jnp.concatenate([re, im], axis=1), waves_ref, 1)
     re, im = (y[:, :LANES], y[:, LANES:])
     re, im = (re * cosine - im * sine, re * sine + im * cosine)
-    y = from_right(jnp.concatenate([re, im], axis=1), back_ref[...])
+    y = from_right(jnp.concatenate([re, im], axis=1), waves_ref, 2)
     re, im = (y[:, :LANES], y[:, LANES:])
     re, im = (re * small_re + im * small_im, im * small_re - re * small_im)
-    out_ref[...] = from_left(leave_ref[...], jnp.concatenate([re, im], axis=0))
+    out_ref[...] = from_left(waves_ref, 3, jnp.concatenate([re, im], axis=0))
 
 
 def one_hot(row, count):
@@ -323,25 +309,10 @@
     return jax.ShapeDtypeStruct((count, LANES), F32)
 
 
-def picked(kernel, index, array, table, tail):
-    zeros = (0,) * len(tail)
-    return pl.pallas_call(
-        kernel,
-        out_shape=rows_of(array.shape[0]),
-        grid_spec=pltpu.PrefetchScalarGridSpec(
-            num_scalar_prefetch=1,
-            grid=(1,),
-            in_specs=[
-                pl.BlockSpec(array.shape, lambda i, at: (0, 0)),
-                pl.BlockSpec((1, *tail), lambda i, at: (at[0], *zeros)),
-            ],
-            out_specs=pl.BlockSpec(array.shape, lambda i, at: (0, 0)),
-        ),
-    )(index, array, table)
-
-
 def exchange(array, axes, peers):
-    tiles = array.reshape(peers, array.shape[0] // peers, LANES)
+    rows = array.shape[0] // peers
+    tile = 8 if rows % 8 == 0 else 1
+    tiles = array.reshape(peers, rows // tile, tile, LANES)
     return lax.all_to_all(tiles, axes, 0, 0, tiled=True).reshape(array.shape)
 
 
@@ -350,35 +321,48 @@
     group = lax.axis_index("mode").astype(jnp.int32)[None]
     th, tl = (lax.axis_index("th"), lax.axis_index("tl"))
     place = jnp.stack([th, tl]).astype(jnp.int32)
-    low_place = tl.astype(jnp.int32)[None]
-    whole_place = (th * 4 + tl).astype(jnp.int32)[None]
+    entry = lax.dynamic_index_in_dim(tables["entry"], tl, keepdims=False)
+    middle = lax.dynamic_index_in_dim(tables["middle"], th * 4 + tl, keepdims=False)
     weights = intersections.reshape(1, -1)
     along, across = (("th", "tl"), "mode")
     vmem = pl.BlockSpec(memory_space=pltpu.VMEM)
     smem = pl.BlockSpec(memory_space=pltpu.SMEM)
-    limit = pltpu.CompilerParams(vmem_limit_bytes=48 * 1024 * 1024)
-
-    def spectral(state, into):
+    limit = pltpu.CompilerParams(vmem_limit_bytes=16 * 1024 * 1024)
+
+    def picked(kernel, state, table):
+        return pl.pallas_call(
+            kernel,
+            out_shape=rows_of(256),
+            in_specs=[vmem, vmem],
+            out_specs=vmem,
+            compiler_params=limit,
+        )(state, table)
+
+    def spectral(state):
         return pl.pallas_call(
             spectral_kernel,
             out_shape=rows_of(256),
-            in_specs=[smem, smem] + [vmem] * 6,
+            in_specs=[smem, smem] + [vmem] * 3,
             out_specs=vmem,
             compiler_params=limit,
-        )(place, beta, state, into, tables["ahead"], tables["back"], tables["leave"], tables["small"])
+        )(place, beta, state, tables["waves"], tables["small"])
 
     state = pl.pallas_call(
-        enter_kernel, out_shape=rows_of(256), in_specs=[vmem], out_specs=vmem
+        enter_kernel,
+        out_shape=rows_of(256),
+        in_specs=[vmem],
+        out_specs=vmem,
+        compiler_params=limit,
     )(field)
     state = exchange(state, along, 16)
-    state = picked(first_radix_kernel, low_place, state, tables["entry"], (4, 3, 2, 8, LANES))
+    state = picked(first_radix_kernel, state, entry)
     state = exchange(state, "tl", 4)
     norms = []
     for step in range(STEPS):
         last = step == STEPS - 1
-        state = spectral(state, tables["later" if step else "first"])
+        state = spectral(state)
         state = exchange(state, along, 16)
-        state = picked(back_kernel, whole_place, state, tables["middle"], (3, 2, 8, LANES))
+        state = picked(back_kernel, state, middle)
         state = exchange(state, across, 32)
         out = pl.pallas_call(
             functools.partial(kerr_kernel, last),
@@ -394,10 +378,14 @@
         state, norm = out
         norms.append(norm)
         state = exchange(state, across, 32)
-        state = picked(ahead_kernel, whole_place, state, tables["middle"], (3, 2, 8, LANES))
+        state = picked(ahead_kernel, state, middle)
         state = exchange(state, along, 16)
     state = pl.pallas_call(
-        regroup_kernel, out_shape=rows_of(272), in_specs=[smem, vmem], out_specs=vmem
+        regroup_kernel,
+        out_shape=rows_of(272),
+        in_specs=[smem, vmem],
+        out_specs=vmem,
+        compiler_params=limit,
     )(group, state)
     state = exchange(state, along, 16)
     return pl.pallas_call(
@@ -408,6 +396,7 @@
         ),
         in_specs=[vmem],
         out_specs=(vmem, vmem),
+        compiler_params=limit,
     )(state)
 
 

time: 193 us -> 176 us (0.912)
  Pallas kernels: 20 us -> 11.6 us
  blocking collectives: 96.3 us -> 93 us
  local copies, waits for them, and re-layouts: 5.32 us -> 2.65 us
  waiting for transfers between devices: 40.9 us -> 38.6 us
    pallas_call x4, Pallas kernels: 6.52 us -> 0.78 us  [picked(): pl.pallas_call(kernel, out_shape=rows_of(256), in_specs=[vmem, vmem], out...]
    all_to_all x6, blocking collectives: 96.3 us -> 93 us  [exchange(): return lax.all_to_all(tiles, axes, 0, 0, tiled=True).reshape(array.shape)]
    reshape x4 -> x0, local copies, waits for them, and re-layouts: 2.99 us -> none  [the longest x2 1.63 us: exchange(): tiles = array.reshape(peers, array.shape[0] // peers, LANES)]
    all_to_all x4, waiting for transfers between devices: 40.9 us -> 38.6 us  [exchange(): return lax.all_to_all(tiles, axes, 0, 0, tiled=True).reshape(array.shape)]
  transfers between devices with their start and end apart: 4 -> 4, of which waited for: 4 -> 4; matrix products, arithmetic and copies ran while one was open for 0% -> 1% of each run, Pallas kernels for 0% -> 0%
where the time goes in v1:
time: 176 us; the launch traced here: 175 us
  blocking collectives  93 us (53%)
  waiting for transfers between devices  38.6 us (22%)
  starting transfers between devices  28.7 us (16%)
  Pallas kernels  11.6 us (7%)
  local copies, waits for them, and re-layouts  2.65 us (2%)
    all_to_all x6, blocking collectives, exchange(): return lax.all_to_all(tiles, axes, 0, 0, tiled=True).reshape(array.shape)  93 us
    all_to_all x4, waiting for transfers between devices, exchange(): return lax.all_to_all(tiles, axes, 0, 0, tiled=True).reshape(array.shape)  38.6 us
    all_to_all x4, starting transfers between devices, exchange(): return lax.all_to_all(tiles, axes, 0, 0, tiled=True).reshape(array.shape)  28.7 us
    pallas_call x2, Pallas kernels, shards(): pl.pallas_call(functools.partial(kerr_kernel, last), out_shape=rows_of(38...  5.39 us
    pallas_call x2, Pallas kernels, spectral(): pl.pallas_call(spectral_kernel, out_shape=rows_of(256), in_specs=[smem, s...  3.71 us
  transfers between devices with their start and end apart: 4, of which 4 were waited for; matrix products, arithmetic and copies ran while one was open for 1% of the time, Pallas kernels for 0%

profile of v1, /device:TPU:32, one launch (start us, length us, event | category | flops | bytes accessed | tf_op | source)
XLA Modules:
  0.0 175.3 jit_solution(5971656214459180775)
XLA Ops:
  0.7 1.0 copy-done.2
  1.6 0.7 shard_map.95
  2.4 15.2 %all-to-all-start = ((f32[16,2,8,128]{3,2,1,0:T(8,128)}), f32[16,2,8,128]{3,2,1,0:T(8,128)S(1)}, u32[]{:S(2)}, u32[]{:S(2)}) async-start(f32[16,2,8,128]{3,2,1,0:T(8,128)} %bitcast.3), calls=%async_computation | async-start | bytes 262144 | tf_op jit(solution)/shard_map/all_to_all | solution.py:316
  17.6 0.9 dynamic-slice_bitcast_fusion.twist_ref
  18.5 13.3 %all-to-all-done = f32[16,2,8,128]{3,2,1,0:T(8,128)S(1)} async-done(((f32[16,2,8,128]{3,2,1,0:T(8,128)}), f32[16,2,8,128]{3,2,1,0:T(8,128)S(1)}, u32[]{:S(2)}, u32[]{:S(2)}) %all-to-all-start) | async-done | bytes 131104 | tf_op jit(solution)/shard_map/all_to_all | solution.py:316
  31.8 0.7 shard_map.96
  32.5 4.0 %all-to-all-start.1 = ((f32[4,8,8,128]{3,2,1,0:T(8,128)}), f32[4,8,8,128]{3,2,1,0:T(8,128)S(1)}, u32[]{:S(2)}, u32[]{:S(2)}) async-start(f32[4,8,8,128]{3,2,1,0:T(8,128)} %bitcast.6), calls=%async_computation.1 | async-start | bytes 262144 | tf_op jit(solution)/shard_map/all_to_all | solution.py:316
  36.6 5.1 %all-to-all-done.1 = f32[4,8,8,128]{3,2,1,0:T(8,128)S(1)} async-done(((f32[4,8,8,128]{3,2,1,0:T(8,128)}), f32[4,8,8,128]{3,2,1,0:T(8,128)S(1)}, u32[]{:S(2)}, u32[]{:S(2)}) %all-to-all-start.1) | async-done | bytes 131104 | tf_op jit(solution)/shard_map/all_to_all | solution.py:316
  41.7 2.2 %shard_map.97 = f32[256,128]{1,0:T(8,128)} custom-call(s32[2]{0:T(128)S(1)} %pad_add_fusion.place_ref, f32[3,4]{1,0:T(4,128)S(1)} %copy-done.5, f32[256,128]{1,0:T(8,128)S(1)} %bitcast.46, bf16[4,2,256,256]{3,2,1,0:T(8,128)(2,1)S(1)} %copy-done, f32[2,128,128]{2,1,0:T(8,128)S(1)} %copy-done.1), custom_call_target="tpu_custom_call" | custom-call | tf_op jit(solution)/shard_map/pallas_call | solution.py:342
  43.9 5.6 %all-to-all-start.2 = ((f32[16,2,8,128]{3,2,1,0:T(8,128)}), f32[16,2,8,128]{3,2,1,0:T(8,128)S(1)}, u32[]{:S(2)}, u32[]{:S(2)}) async-start(f32[16,2,8,128]{3,2,1,0:T(8,128)} %bitcast.8), calls=%async_computation.2 | async-start | bytes 262144 | tf_op jit(solution)/shard_map/all_to_all | solution.py:316
  49.5 0.7 dynamic-slice_bitcast_fusion.1.twist_ref
  50.2 12.0 %all-to-all-done.2 = f32[16,2,8,128]{3,2,1,0:T(8,128)S(1)} async-done(((f32[16,2,8,128]{3,2,1,0:T(8,128)}), f32[16,2,8,128]{3,2,1,0:T(8,128)S(1)}, u32[]{:S(2)}, u32[]{:S(2)}) %all-to-all-start.2) | async-done | bytes 131104 | tf_op jit(solution)/shard_map/all_to_all | solution.py:316
  62.3 14.9 %all_to_all.50 = f32[32,1,8,128]{3,2,1,0:T(8,128)S(1)} all-to-all(f32[32,1,8,128]{3,2,1,0:T(8,128)S(1)} %bitcast.41), channel_id=1, replica_groups=mesh['mode'=32,'th'=4,'tl'=4] {'mode'}, dimensions={0} | all-to-all | bytes 262144 | tf_op jit(solution)/shard_map/all_to_all | solution.py:316
  77.2 2.3 %shard_map.99 = (f32[256,128]{1,0:T(8,128)S(1)}, f32[8,128]{1,0:T(8,128)S(1)}) custom-call(f32[256,128]{1,0:T(8,128)S(1)} %bitcast.38, s32[4,1024]{1,0:T(4,128)S(1)} %copy-done.3, f32[1,1024]{1,0:T(1,128)S(1)} %bitcast.50), custom_call_target="tpu_custom_call" | custom-call | tf_op jit(solution)/shard_map/pallas_call | solution.py:367
  79.5 11.3 %all_to_all.51 = f32[32,1,8,128]{3,2,1,0:T(8,128)S(1)} all-to-all(f32[32,1,8,128]{3,2,1,0:T(8,128)S(1)} %bitcast.49), channel_id=1, replica_groups=mesh['mode'=32,'th'=4,'tl'=4] {'mode'}, dimensions={0} | all-to-all | bytes 262144 | tf_op jit(solution)/shard_map/all_to_all | solution.py:316
  90.9 18.1 %all_to_all.52 = f32[16,2,8,128]{3,2,1,0:T(8,128)S(1)} all-to-all(f32[16,2,8,128]{3,2,1,0:T(8,128)S(1)} %bitcast.43), channel_id=1, replica_groups=mesh['mode'=32,'th'=4,'tl'=4] {'th','tl'}, dimensions={0} | all-to-all | bytes 262144 | tf_op jit(solution)/shard_map/all_to_all | solution.py:316
  109.0 1.5 shard_map.101
  110.5 19.1 %all_to_all.53 = f32[16,2,8,128]{3,2,1,0:T(8,128)S(1)} all-to-all(f32[16,2,8,128]{3,2,1,0:T(8,128)S(1)} %bitcast.48), channel_id=1, replica_groups=mesh['mode'=32,'th'=4,'tl'=4] {'th','tl'}, dimensions={0} | all-to-all | bytes 262144 | tf_op jit(solution)/shard_map/all_to_all | solution.py:316
  129.7 11.1 %all_to_all.54 = f32[32,1,8,128]{3,2,1,0:T(8,128)S(1)} all-to-all(f32[32,1,8,128]{3,2,1,0:T(8,128)S(1)} %bitcast.40), channel_id=1, replica_groups=mesh['mode'=32,'th'=4,'tl'=4] {'mode'}, dimensions={0} | all-to-all | bytes 262144 | tf_op jit(solution)/shard_map/all_to_all | solution.py:316
  140.8 3.1 %shard_map.103 = f32[384,128]{1,0:T(8,128)} custom-call(f32[256,128]{1,0:T(8,128)S(1)} %bitcast.45, s32[4,1024]{1,0:T(4,128)S(1)} %copy-done.3, f32[1,1024]{1,0:T(1,128)S(1)} %bitcast.51, f32[8,128]{1,0:T(8,128)S(1)} %get-tuple-element.5.refs_0_), custom_call_target="tpu_custom_call" | custom-call | tf_op jit(solution)/shard_map/pallas_call | solution.py:367
  143.9 3.9 %all-to-all-start.8 = ((f32[32,12,1,128]{3,2,1,0:T(1,128)}), f32[32,12,1,128]{3,2,1,0:T(1,128)S(1)}, u32[]{:S(2)}, u32[]{:S(2)}) async-start(f32[32,12,1,128]{3,2,1,0:T(1,128)} %bitcast.25), calls=%async_computation.8 | async-start | bytes 393216 | tf_op jit(solution)/shard_map/all_to_all | solution.py:316
  147.8 8.2 %all-to-all-done.8 = f32[32,12,1,128]{3,2,1,0:T(1,128)S(1)} async-done(((f32[32,12,1,128]{3,2,1,0:T(1,128)}), f32[32,12,1,128]{3,2,1,0:T(1,128)S(1)}, u32[]{:S(2)}, u32[]{:S(2)}) %all-to-all-start.8) | async-done | bytes 196640 | tf_op jit(solution)/shard_map/all_to_all | solution.py:316
  156.1 18.4 %all_to_all.55 = f32[16,17,1,128]{3,2,1,0:T(1,128)S(1)} all-to-all(f32[16,17,1,128]{3,2,1,0:T(1,128)S(1)} %bitcast.36), channel_id=1, replica_groups=mesh['mode'=32,'th'=4,'tl'=4] {'th','tl'}, dimensions={0} | all-to-all | bytes 278528 | tf_op jit(solution)/shard_map/all_to_all | solution.py:316
  174.5 0.8 shard_map.105
  (16 shorter events, 0.4 us)
Async XLA Ops:
  0.6 41.0 %copy-start = (bf16[4,2,256,256]{3,2,1,0:T(8,128)(2,1)S(1)}, bf16[4,2,256,256]{3,2,1,0:T(8,128)(2,1)}, u32[]{:S(2)}) copy-start(bf16[4,2,256,256]{3,2,1,0:T(8,128)(2,1)} %constant.33.clone.waves_ref) | copy-start | bytes 3145732
  0.6 1.0 copy-start.2
  2.4 29.4 %all-to-all-start = ((f32[16,2,8,128]{3,2,1,0:T(8,128)}), f32[16,2,8,128]{3,2,1,0:T(8,128)S(1)}, u32[]{:S(2)}, u32[]{:S(2)}) async-start(f32[16,2,8,128]{3,2,1,0:T(8,128)} %bitcast.3), calls=%async_computation | async-start | bytes 262144 | tf_op jit(solution)/shard_map/all_to_all | solution.py:316
  32.5 9.2 %copy-start.1 = (f32[2,128,128]{2,1,0:T(8,128)S(1)}, f32[2,128,128]{2,1,0:T(8,128)}, u32[]{:S(2)}) copy-start(f32[2,128,128]{2,1,0:T(8,128)} %constant.34.clone.small_ref) | copy-start | bytes 393220
  32.5 9.2 %all-to-all-start.1 = ((f32[4,8,8,128]{3,2,1,0:T(8,128)}), f32[4,8,8,128]{3,2,1,0:T(8,128)S(1)}, u32[]{:S(2)}, u32[]{:S(2)}) async-start(f32[4,8,8,128]{3,2,1,0:T(8,128)} %bitcast.6), calls=%async_computation.1 | async-start | bytes 262144 | tf_op jit(solution)/shard_map/all_to_all | solution.py:316
  36.5 5.2 %copy-start.5 = (f32[3,4]{1,0:T(4,128)S(1)}, f32[3,4]{1,0:T(4,128)}, u32[]{:S(2)}) copy-start(f32[3,4]{1,0:T(4,128)} %beta_ref.3) | copy-start | bytes 148
  43.9 18.4 %all-to-all-start.2 = ((f32[16,2,8,128]{3,2,1,0:T(8,128)}), f32[16,2,8,128]{3,2,1,0:T(8,128)S(1)}, u32[]{:S(2)}, u32[]{:S(2)}) async-start(f32[16,2,8,128]{3,2,1,0:T(8,128)} %bitcast.8), calls=%async_computation.2 | async-start | bytes 262144 | tf_op jit(solution)/shard_map/all_to_all | solution.py:316
  62.3 14.9 %copy-start.3 = (s32[4,1024]{1,0:T(4,128)S(1)}, s32[4,1024]{1,0:T(4,128)}, u32[]{:S(2)}) copy-start(s32[4,1024]{1,0:T(4,128)} %quartets_ref.3) | copy-start | bytes 49156
  62.3 14.9 %copy-start.4 = (f32[1024]{0:T(1024)S(1)}, f32[1024]{0:T(1024)}, u32[]{:S(2)}) copy-start(f32[1024]{0:T(1024)} %param.11) | copy-start | bytes 12292
  143.9 12.1 %all-to-all-start.8 = ((f32[32,12,1,128]{3,2,1,0:T(1,128)}), f32[32,12,1,128]{3,2,1,0:T(1,128)S(1)}, u32[]{:S(2)}, u32[]{:S(2)}) async-start(f32[32,12,1,128]{3,2,1,0:T(1,128)} %bitcast.25), calls=%async_computation.8 | async-start | bytes 393216 | tf_op jit(solution)/shard_map/all_to_all | solution.py:316

commit v2 on v1

--- a/solution.py
+++ b/solution.py
@@ -28,7 +28,7 @@
 
 
 @functools.cache
-def host_tables():
+def host_waves():
     index = np.arange(LANES)
     wave = np.exp(-2j * math.pi / LANES * (index[:, None] * index[None, :] % LANES))
     ahead = np.block([[wave.real, -wave.imag], [wave.imag, wave.real]])
@@ -40,31 +40,8 @@
     tile_order = row_order(
         [(v * 16 + w, ri) for w in range(16) for ri in range(2) for v in range(8)]
     )
-    small = np.exp(-2j * math.pi / QUARTER * (index[:, None] * index[None, :] % QUARTER))
-
-    def twist(place):
-        angles = np.arange(4)[1:, None, None] * place[None]
-        turned = np.exp(-2j * math.pi / TIME * (angles % TIME))
-        return np.stack([turned.real, turned.imag], axis=1)
-
-    rest = np.array([v0 * 2048 + w * LANES for v0 in range(2) for w in range(4)])
-    rest = rest[:, None] + index[None, :]
-    entry = np.stack(
-        [np.stack([twist(v2 * 4096 + zb * 512 + rest) for v2 in range(4)]) for zb in range(4)]
-    )
-    v = np.arange(8)[:, None] * 2048 + index[None, :]
-    middle = np.stack([twist(v + w * LANES) for w in range(16)])
-    return {
-        "waves": np.stack(
-            [
-                two_parts(table)
-                for table in (ahead[:, tile_order], ahead.T, back.T, back[tile_order] / TIME)
-            ]
-        ),
-        "small": np.stack([small.real, small.imag]).astype(np.float32),
-        "entry": entry.astype(np.float32),
-        "middle": middle.astype(np.float32),
-    }
+    tables = (ahead[:, tile_order], ahead.T, back.T, back[tile_order] / TIME)
+    return np.stack([two_parts(table) for table in tables])
 
 
 def split(array):
@@ -88,6 +65,45 @@
     return dot(high, waves_ref[which, 0]) + (
         dot(low, waves_ref[which, 0]) + dot(high, waves_ref[which, 1])
     )
+
+
+def small_cosine_and_sine(x):
+    z = x * x
+    sine = ((-1.9515295891e-4 * z + 8.3321608736e-3) * z - 1.6666654611e-1) * z * x + x
+    cosine = (
+        (2.443315711809948e-5 * z - 1.388731625493765e-3) * z + 4.166664568298827e-2
+    ) * z * z - 0.5 * z + 1.0
+    return (cosine, sine)
+
+
+def in_quarter(turns, cosine, sine):
+    quarter = turns & 3
+    odd = (quarter & 1) == 1
+    c = jnp.where(odd, sine, cosine)
+    s = jnp.where(odd, cosine, sine)
+    c = jnp.where((quarter == 1) | (quarter == 2), -c, c)
+    s = jnp.where(quarter >= 2, -s, s)
+    return (c, s)
+
+
+def cosine_and_sine(angle):
+    scaled = angle * (2.0 / math.pi)
+    turns = (scaled + jnp.where(scaled >= 0.0, 0.5, -0.5)).astype(jnp.int32)
+    count = turns.astype(F32)
+    x = angle - count * 1.5703125
+    x = x - count * 4.837512969970703125e-4
+    x = x - count * 7.5497899548918822e-8
+    return in_quarter(turns, *small_cosine_and_sine(x))
+
+
+def twist(number):
+    turns = (number + TIME // 8) // QUARTER
+    rest = (number - turns * QUARTER).astype(F32)
+    return in_quarter(turns, *small_cosine_and_sine(rest * (2.0 * math.pi / TIME)))
+
+
+def row_and_lane():
+    return (lax.broadcasted_iota(jnp.int32, (8, LANES), axis) for axis in range(2))
 
 
 def enter_kernel(field_ref, out_ref):
@@ -111,22 +127,37 @@
     return [out[0], out[3], out[2], out[1]]
 
 
-def first_radix_kernel(x_ref, twist_ref, out_ref):
+def turned_back(pair, c, s):
+    re, im = pair
+    return (re * c + im * s, im * c - re * s)
+
+
+def turned(pair, c, s):
+    return turned_back(pair, c, -s)
+
+
+def first_radix_kernel(zb_ref, x_ref, out_ref):
+    row, lane = row_and_lane()
+    place = (row // 4) * 2048 + (row % 4) * LANES + lane + zb_ref[0] * 512
     for v2 in range(4):
         at = [a * 64 + v2 * 16 for a in range(4)]
         y = radix_ahead([(x_ref[b : b + 8, :], x_ref[b + 8 : b + 16, :]) for b in at])
         for f in range(4):
-            re, im = y[f]
-            if f:
-                c, s = twist_ref[v2, f - 1, 0], twist_ref[v2, f - 1, 1]
-                re, im = (re * c - im * s, re * s + im * c)
-            for ri, part in enumerate((re, im)):
+            pair = turned_back(y[f], *twist(f * (place + v2 * 4096))) if f else y[f]
+            for ri in range(2):
                 for v0 in range(2):
                     first = f * 64 + ri * 8 + v2 * 2 + v0
-                    out_ref[pl.ds(first, 4, stride=16), :] = part[v0 * 4 : v0 * 4 + 4]
-
-
-def ahead_kernel(x_ref, twist_ref, out_ref):
+                    out_ref[pl.ds(first, 4, stride=16), :] = pair[ri][v0 * 4 : v0 * 4 + 4]
+
+
+def middle_twists(th_ref, tl_ref):
+    row, lane = row_and_lane()
+    place = row * 2048 + lane + (th_ref[0] * 4 + tl_ref[0]) * LANES
+    return [None] + [twist(f * place) for f in range(1, 4)]
+
+
+def ahead_kernel(th_ref, tl_ref, x_ref, out_ref):
+    twists = middle_twists(th_ref, tl_ref)
     for low in range(4):
         y = radix_ahead(
             [
@@ -135,62 +166,32 @@
             ]
         )
         for f in range(4):
-            re, im = y[f]
-            if f:
-                c, s = twist_ref[f - 1, 0], twist_ref[f - 1, 1]
-                re, im = (re * c - im * s, re * s + im * c)
+            re, im = turned_back(y[f], *twists[f]) if f else y[f]
             at = low * 64 + f * 16
             out_ref[at : at + 8, :] = re
             out_ref[at + 8 : at + 16, :] = im
 
 
-def back_kernel(x_ref, twist_ref, out_ref):
+def back_kernel(th_ref, tl_ref, x_ref, out_ref):
+    twists = middle_twists(th_ref, tl_ref)
     for low in range(4):
         y = []
         for f in range(4):
             at = low * 64 + f * 16
-            re, im = (x_ref[at : at + 8, :], x_ref[at + 8 : at + 16, :])
-            if f:
-                c, s = twist_ref[f - 1, 0], twist_ref[f - 1, 1]
-                re, im = (re * c + im * s, im * c - re * s)
-            y.append((re, im))
+            pair = (x_ref[at : at + 8, :], x_ref[at + 8 : at + 16, :])
+            y.append(turned(pair, *twists[f]) if f else pair)
         for a, pair in enumerate(radix_back(y)):
             for ri in range(2):
                 out_ref[pl.ds(a * 64 + low * 2 + ri, 8, stride=8), :] = pair[ri]
 
 
-def cosine_and_sine(angle):
-    scaled = angle * (2.0 / math.pi)
-    turns = (scaled + jnp.where(scaled >= 0.0, 0.5, -0.5)).astype(jnp.int32)
-    count = turns.astype(F32)
-    x = angle - count * 1.5703125
-    x = x - count * 4.837512969970703125e-4
-    x = x - count * 7.5497899548918822e-8
-    z = x * x
-    sine = ((-1.9515295891e-4 * z + 8.3321608736e-3) * z - 1.6666654611e-1) * z * x + x
-    cosine = (
-        (2.443315711809948e-5 * z - 1.388731625493765e-3) * z + 4.166664568298827e-2
-    ) * z * z - 0.5 * z + 1.0
-    quarter = turns & 3
-    odd = (quarter & 1) == 1
-    c = jnp.where(odd, sine, cosine)
-    s = jnp.where(odd, cosine, sine)
-    c = jnp.where((quarter == 1) | (quarter == 2), -c, c)
-    s = jnp.where(quarter >= 2, -s, s)
-    return (c, s)
-
-
-def spectral_kernel(
-    place_ref, beta_ref, x_ref, waves_ref, small_ref, out_ref
-):
-    low, f = (place_ref[0], place_ref[1])
+def spectral_kernel(th_ref, tl_ref, beta_ref, x_ref, waves_ref, out_ref):
+    low, f = (th_ref[0], tl_ref[0])
     offset, slope, curve = (beta_ref[k, low] for k in range(3))
     shape = (LANES, LANES)
-    wave = 4 * (
-        lax.broadcasted_iota(jnp.int32, shape, 0)
-        + LANES * lax.broadcasted_iota(jnp.int32, shape, 1)
-    )
-    wave = wave + f
+    row, lane = (lax.broadcasted_iota(jnp.int32, shape, axis) for axis in range(2))
+    small = twist(4 * row * lane)
+    wave = 4 * (row + LANES * lane) + f
     signed = jnp.where(wave < TIME // 2, wave, wave - TIME)
     frequency = signed.astype(F32) * (1.0 / (TIME / 2))
     angle = (
@@ -199,17 +200,13 @@
         + 3000.0 * curve * frequency * frequency
     )
     cosine, sine = cosine_and_sine(angle)
-    small_re, small_im = (small_ref[0], small_ref[1])
 
     y = from_left(waves_ref, 0, x_ref[...])
-    re, im = (y[:LANES], y[LANES:])
-    re, im = (re * small_re - im * small_im, re * small_im + im * small_re)
+    re, im = turned_back((y[:LANES], y[LANES:]), *small)
     y = from_right(jnp.concatenate([re, im], axis=1), waves_ref, 1)
-    re, im = (y[:, :LANES], y[:, LANES:])
-    re, im = (re * cosine - im * sine, re * sine + im * cosine)
+    re, im = turned((y[:, :LANES], y[:, LANES:]), cosine, sine)
     y = from_right(jnp.concatenate([re, im], axis=1), waves_ref, 2)
-    re, im = (y[:, :LANES], y[:, LANES:])
-    re, im = (re * small_re + im * small_im, im * small_re - re * small_im)
+    re, im = turned((y[:, :LANES], y[:, LANES:]), *small)
     out_ref[...] = from_left(waves_ref, 3, jnp.concatenate([re, im], axis=0))
 
 
@@ -317,35 +314,34 @@
 
 
 def shards(field, beta, quartets, intersections):
-    tables = {name: jnp.asarray(value) for name, value in host_tables().items()}
-    group = lax.axis_index("mode").astype(jnp.int32)[None]
-    th, tl = (lax.axis_index("th"), lax.axis_index("tl"))
-    place = jnp.stack([th, tl]).astype(jnp.int32)
-    entry = lax.dynamic_index_in_dim(tables["entry"], tl, keepdims=False)
-    middle = lax.dynamic_index_in_dim(tables["middle"], th * 4 + tl, keepdims=False)
+    waves = jnp.asarray(host_waves())
+    field, group, th, tl = lax.optimization_barrier(
+        (field, *(lax.axis_index(a).astype(jnp.int32) for a in ("mode", "th", "tl")))
+    )
+    group, th, tl = (group[None], th[None], tl[None])
     weights = intersections.reshape(1, -1)
     along, across = (("th", "tl"), "mode")
     vmem = pl.BlockSpec(memory_space=pltpu.VMEM)
     smem = pl.BlockSpec(memory_space=pltpu.SMEM)
     limit = pltpu.CompilerParams(vmem_limit_bytes=16 * 1024 * 1024)
 
-    def picked(kernel, state, table):
+    def placed(kernel, state, *numbers):
         return pl.pallas_call(
             kernel,
             out_shape=rows_of(256),
-            in_specs=[vmem, vmem],
+            in_specs=[smem] * len(numbers) + [vmem],
             out_specs=vmem,
             compiler_params=limit,
-        )(state, table)
+        )(*numbers, state)
 
     def spectral(state):
         return pl.pallas_call(
             spectral_kernel,
             out_shape=rows_of(256),
-            in_specs=[smem, smem] + [vmem] * 3,
+            in_specs=[smem] * 3 + [vmem] * 2,
             out_specs=vmem,
             compiler_params=limit,
-        )(place, beta, state, tables["waves"], tables["small"])
+        )(th, tl, beta, state, waves)
 
     state = pl.pallas_call(
         enter_kernel,
@@ -355,14 +351,14 @@
         compiler_params=limit,
     )(field)
     state = exchange(state, along, 16)
-    state = picked(first_radix_kernel, state, entry)
+    state = placed(first_radix_kernel, state, tl)
     state = exchange(state, "tl", 4)
     norms = []
     for step in range(STEPS):
         last = step == STEPS - 1
         state = spectral(state)
         state = exchange(state, along, 16)
-        state = picked(back_kernel, state, middle)
+        state = placed(back_kernel, state, th, tl)
         state = exchange(state, across, 32)
         out = pl.pallas_call(
             functools.partial(kerr_kernel, last),
@@ -378,7 +374,7 @@
         state, norm = out
         norms.append(norm)
         state = exchange(state, across, 32)
-        state = picked(ahead_kernel, state, middle)
+        state = placed(ahead_kernel, state, th, tl)
         state = exchange(state, along, 16)
     state = pl.pallas_call(
         regroup_kernel,

time: 176 us -> 173 us (0.983)
  blocking collectives: 93 us -> 161 us
  waiting for transfers between devices: 38.6 us -> 0 us
  starting transfers between devices: 28.7 us -> 0 us
  Pallas kernels: 11.6 us -> 9.11 us
    all_to_all x6 -> x10, blocking collectives: 93 us -> 161 us  [exchange(): return lax.all_to_all(tiles, axes, 0, 0, tiled=True).reshape(array.shape)]
    all_to_all x4 -> x0, waiting for transfers between devices: 38.6 us -> none  [exchange(): return lax.all_to_all(tiles, axes, 0, 0, tiled=True).reshape(array.shape)]
    all_to_all x4 -> x0, starting transfers between devices: 28.7 us -> none  [exchange(): return lax.all_to_all(tiles, axes, 0, 0, tiled=True).reshape(array.shape)]
  transfers between devices with their start and end apart: 4 -> 0, of which waited for: 4 -> 0; matrix products, arithmetic and copies ran while one was open for 1% -> 0% of each run, Pallas kernels for 0% -> 0%
where the time goes in v2:
time: 173 us; the launch traced here: 172 us
  blocking collectives  161 us (93%)
  Pallas kernels  9.11 us (5%)
    all_to_all x10, blocking collectives, exchange(): return lax.all_to_all(tiles, axes, 0, 0, tiled=True).reshape(array.shape)  161 us
    pallas_call x2, Pallas kernels, shards(): pl.pallas_call(functools.partial(kerr_kernel, last), out_shape=rows_of(38...  4.71 us

profile of v2, /device:TPU:32, one launch (start us, length us, event | category | flops | bytes accessed | tf_op | source)
XLA Modules:
  0.0 172.4 jit_solution(9215419464621809022)
XLA Ops:
  0.6 0.0 copy-start
  0.7 1.0 copy-done.1
  1.6 0.1 shard_map.68
  1.7 29.2 %all_to_all.50 = f32[16,2,8,128]{3,2,1,0:T(8,128)S(1)} all-to-all(f32[16,2,8,128]{3,2,1,0:T(8,128)S(1)} %bitcast.47), channel_id=1, replica_groups=mesh['mode'=32,'th'=4,'tl'=4] {'th','tl'}, dimensions={0} | all-to-all | bytes 262144 | tf_op jit(solution)/shard_map/all_to_all | solution.py:313
  30.9 0.1 shard_map.69
  31.1 8.8 %all_to_all.51 = f32[4,8,8,128]{3,2,1,0:T(8,128)S(1)} all-to-all(f32[4,8,8,128]{3,2,1,0:T(8,128)S(1)} %bitcast.42), channel_id=1, replica_groups=mesh['mode'=32,'th'=4,'tl'=4] {'tl'}, dimensions={0} | all-to-all | bytes 262144 | tf_op jit(solution)/shard_map/all_to_all | solution.py:313
  39.9 0.7 copy-done.4
  40.6 1.5 shard_map.70
  42.2 18.2 %all_to_all.52 = f32[16,2,8,128]{3,2,1,0:T(8,128)S(1)} all-to-all(f32[16,2,8,128]{3,2,1,0:T(8,128)S(1)} %bitcast.37), channel_id=1, replica_groups=mesh['mode'=32,'th'=4,'tl'=4] {'th','tl'}, dimensions={0} | all-to-all | bytes 262144 | tf_op jit(solution)/shard_map/all_to_all | solution.py:313
  60.3 0.1 shard_map.71
  60.4 14.9 %all_to_all.53 = f32[32,1,8,128]{3,2,1,0:T(8,128)S(1)} all-to-all(f32[32,1,8,128]{3,2,1,0:T(8,128)S(1)} %bitcast.44), channel_id=1, replica_groups=mesh['mode'=32,'th'=4,'tl'=4] {'mode'}, dimensions={0} | all-to-all | bytes 262144 | tf_op jit(solution)/shard_map/all_to_all | solution.py:313
  75.3 2.4 %shard_map.72 = (f32[256,128]{1,0:T(8,128)S(1)}, f32[8,128]{1,0:T(8,128)S(1)}) custom-call(f32[256,128]{1,0:T(8,128)S(1)} %bitcast.38, s32[4,1024]{1,0:T(4,128)S(1)} %copy-done.2, f32[1,1024]{1,0:T(1,128)S(1)} %bitcast.50), custom_call_target="tpu_custom_call" | custom-call | tf_op jit(solution)/shard_map/pallas_call | solution.py:363
  77.7 11.3 %all_to_all.54 = f32[32,1,8,128]{3,2,1,0:T(8,128)S(1)} all-to-all(f32[32,1,8,128]{3,2,1,0:T(8,128)S(1)} %bitcast.49), channel_id=1, replica_groups=mesh['mode'=32,'th'=4,'tl'=4] {'mode'}, dimensions={0} | all-to-all | bytes 262144 | tf_op jit(solution)/shard_map/all_to_all | solution.py:313
  88.9 0.1 shard_map.73
  89.0 18.1 %all_to_all.55 = f32[16,2,8,128]{3,2,1,0:T(8,128)S(1)} all-to-all(f32[16,2,8,128]{3,2,1,0:T(8,128)S(1)} %bitcast.46), channel_id=1, replica_groups=mesh['mode'=32,'th'=4,'tl'=4] {'th','tl'}, dimensions={0} | all-to-all | bytes 262144 | tf_op jit(solution)/shard_map/all_to_all | solution.py:313
  107.1 1.5 shard_map.74
  108.7 19.1 %all_to_all.56 = f32[16,2,8,128]{3,2,1,0:T(8,128)S(1)} all-to-all(f32[16,2,8,128]{3,2,1,0:T(8,128)S(1)} %bitcast.35), channel_id=1, replica_groups=mesh['mode'=32,'th'=4,'tl'=4] {'th','tl'}, dimensions={0} | all-to-all | bytes 262144 | tf_op jit(solution)/shard_map/all_to_all | solution.py:313
  127.8 0.1 shard_map.75
  127.9 11.2 %all_to_all.57 = f32[32,1,8,128]{3,2,1,0:T(8,128)S(1)} all-to-all(f32[32,1,8,128]{3,2,1,0:T(8,128)S(1)} %bitcast.40), channel_id=1, replica_groups=mesh['mode'=32,'th'=4,'tl'=4] {'mode'}, dimensions={0} | all-to-all | bytes 262144 | tf_op jit(solution)/shard_map/all_to_all | solution.py:313
  139.0 2.4 %shard_map.76 = f32[384,128]{1,0:T(8,128)S(1)} custom-call(f32[256,128]{1,0:T(8,128)S(1)} %bitcast.48, s32[4,1024]{1,0:T(4,128)S(1)} %copy-done.2, f32[1,1024]{1,0:T(1,128)S(1)} %bitcast.51, f32[8,128]{1,0:T(8,128)S(1)} %get-tuple-element.13.refs_0_), custom_call_target="tpu_custom_call" | custom-call | tf_op jit(solution)/shard_map/pallas_call | solution.py:363
  141.4 11.7 %all_to_all.58 = f32[32,12,1,128]{3,2,1,0:T(1,128)S(1)} all-to-all(f32[32,12,1,128]{3,2,1,0:T(1,128)S(1)} %bitcast.30), channel_id=1, replica_groups=mesh['mode'=32,'th'=4,'tl'=4] {'mode'}, dimensions={0} | all-to-all | bytes 393216 | tf_op jit(solution)/shard_map/all_to_all | solution.py:313
  153.1 0.2 shard_map.77
  153.2 18.4 %all_to_all.59 = f32[16,17,1,128]{3,2,1,0:T(1,128)S(1)} all-to-all(f32[16,17,1,128]{3,2,1,0:T(1,128)S(1)} %bitcast.33), channel_id=1, replica_groups=mesh['mode'=32,'th'=4,'tl'=4] {'th','tl'}, dimensions={0} | all-to-all | bytes 278528 | tf_op jit(solution)/shard_map/all_to_all | solution.py:313
  171.6 0.8 shard_map.78
  (7 shorter events, 0.0 us)
Async XLA Ops:
  0.6 39.3 %copy-start = (bf16[4,2,256,256]{3,2,1,0:T(8,128)(2,1)S(1)}, bf16[4,2,256,256]{3,2,1,0:T(8,128)(2,1)}, u32[]{:S(2)}) copy-start(bf16[4,2,256,256]{3,2,1,0:T(8,128)(2,1)} %constant.15.clone.waves_ref) | copy-start | bytes 3145732
  0.6 1.0 copy-start.1
  39.9 0.7 copy-start.4
  60.4 15.0 %copy-start.2 = (s32[4,1024]{1,0:T(4,128)S(1)}, s32[4,1024]{1,0:T(4,128)}, u32[]{:S(2)}) copy-start(s32[4,1024]{1,0:T(4,128)} %quartets_ref.3) | copy-start | bytes 49156
  60.4 14.9 %copy-start.3 = (f32[1024]{0:T(1024)S(1)}, f32[1024]{0:T(1024)}, u32[]{:S(2)}) copy-start(f32[1024]{0:T(1024)} %param.8) | copy-start | bytes 12292

commit v3 on v2

--- a/solution.py
+++ b/solution.py
@@ -106,7 +106,23 @@
     return (lax.broadcasted_iota(jnp.int32, (8, LANES), axis) for axis in range(2))
 
 
-def enter_kernel(field_ref, out_ref):
+def rotor_kernel(th_ref, tl_ref, beta_ref, rotor_ref, small_ref):
+    offset, slope, curve = (beta_ref[k, th_ref[0]] for k in range(3))
+    shape = (LANES, LANES)
+    row, lane = (lax.broadcasted_iota(jnp.int32, shape, axis) for axis in range(2))
+    small_ref[0], small_ref[1] = twist(4 * row * lane)
+    wave = 4 * (row + LANES * lane) + tl_ref[0]
+    signed = jnp.where(wave < TIME // 2, wave, wave - TIME)
+    frequency = signed.astype(F32) * (1.0 / (TIME / 2))
+    angle = (
+        math.pi * offset
+        + 300.0 * slope * frequency
+        + 3000.0 * curve * frequency * frequency
+    )
+    rotor_ref[0], rotor_ref[1] = cosine_and_sine(angle)
+
+
+def enter_kernel(field_ref, after_ref, out_ref):
     for ri in range(2):
         for tile in range(32):
             zb, rest = (tile // 4 % 4, tile // 16 * 4 + tile % 4)
@@ -185,55 +201,43 @@
                 out_ref[pl.ds(a * 64 + low * 2 + ri, 8, stride=8), :] = pair[ri]
 
 
-def spectral_kernel(th_ref, tl_ref, beta_ref, x_ref, waves_ref, out_ref):
-    low, f = (th_ref[0], tl_ref[0])
-    offset, slope, curve = (beta_ref[k, low] for k in range(3))
-    shape = (LANES, LANES)
-    row, lane = (lax.broadcasted_iota(jnp.int32, shape, axis) for axis in range(2))
-    small = twist(4 * row * lane)
-    wave = 4 * (row + LANES * lane) + f
-    signed = jnp.where(wave < TIME // 2, wave, wave - TIME)
-    frequency = signed.astype(F32) * (1.0 / (TIME / 2))
-    angle = (
-        math.pi * offset
-        + 300.0 * slope * frequency
-        + 3000.0 * curve * frequency * frequency
-    )
-    cosine, sine = cosine_and_sine(angle)
-
+def spectral_kernel(x_ref, rotor_ref, small_ref, waves_ref, out_ref):
+    rotor = (rotor_ref[0], rotor_ref[1])
+    small = (small_ref[0], small_ref[1])
     y = from_left(waves_ref, 0, x_ref[...])
     re, im = turned_back((y[:LANES], y[LANES:]), *small)
     y = from_right(jnp.concatenate([re, im], axis=1), waves_ref, 1)
-    re, im = turned((y[:, :LANES], y[:, LANES:]), cosine, sine)
+    re, im = turned((y[:, :LANES], y[:, LANES:]), *rotor)
     y = from_right(jnp.concatenate([re, im], axis=1), waves_ref, 2)
     re, im = turned((y[:, :LANES], y[:, LANES:]), *small)
     out_ref[...] = from_left(waves_ref, 3, jnp.concatenate([re, im], axis=0))
 
 
-def one_hot(row, count):
-    ids = lax.broadcasted_iota(jnp.int32, (count, row.shape[1]), 0)
-    return jnp.where(row == ids, 1.0, 0.0).astype(BF16)
-
-
-def kerr_term(fields, quartets_ref, weights_ref):
+def one_hots(quartets_ref, modes):
+    ids = lax.broadcasted_iota(jnp.int32, (modes, quartets_ref.shape[1]), 0)
+    return [
+        jnp.where(quartets_ref[k : k + 1, :] == ids, 1.0, 0.0).astype(BF16) for k in range(4)
+    ]
+
+
+def kerr_term(fields, hot, weights_ref):
     size = fields.shape[0] // 2
     parts = jnp.concatenate(split(fields), axis=1)
     total = None
-    for start in range(0, quartets_ref.shape[1], TILE):
+    for start in range(0, weights_ref.shape[1], TILE):
         here = slice(start, start + TILE)
-        hot = [one_hot(quartets_ref[k : k + 1, here], fields.shape[1]) for k in range(4)]
         (lr, li), (mr, mi), (nr, ni) = (
             (y[:size], y[size:])
-            for y in (dot(parts, jnp.concatenate([hot[k]] * 2, axis=0)) for k in (1, 2, 3))
+            for y in (dot(parts, jnp.concatenate([hot[k][:, here]] * 2, axis=0)) for k in (1, 2, 3))
         )
         weight = weights_ref[:, here]
         pr, pi = (lr * mr - li * mi, lr * mi + li * mr)
         pr, pi = (pr * weight, pi * weight)
-        out_re, out_im = (pr * nr + pi * ni, pi * nr - pr * ni)
-        terms = jnp.concatenate(split(jnp.concatenate([-out_im, out_re], axis=0)), axis=1)
+        terms = jnp.concatenate([pr * ni - pi * nr, pr * nr + pi * ni], axis=0)
+        terms = jnp.concatenate(split(terms), axis=1)
         added = lax.dot_general(
             terms,
-            jnp.concatenate([hot[0]] * 2, axis=1),
+            jnp.concatenate([hot[0][:, here]] * 2, axis=1),
             (((1,), (1,)), ((), ())),
             preferred_element_type=F32,
         )
@@ -246,8 +250,9 @@
     linear = jnp.concatenate(
         [x_ref[pl.ds(ri, modes, stride=2), :].T for ri in range(2)], axis=0
     )
-    first = kerr_term(linear, quartets_ref, weights_ref)
-    second = kerr_term(linear + first, quartets_ref, weights_ref)
+    hot = one_hots(quartets_ref, modes)
+    first = kerr_term(linear, hot, weights_ref)
+    second = kerr_term(linear + first, hot, weights_ref)
     updated = linear + 0.5 * (first + second)
     estimate = 0.5 * (second - first)
     sums = [jnp.sum(y * y, axis=0, keepdims=True) for y in (estimate, updated)]
@@ -261,28 +266,31 @@
     before_ref, out_ref, held_ref = refs
     for ri in range(2):
         held_ref[pl.ds(ri, modes, stride=2), :] = updated[ri * LANES : (ri + 1) * LANES].T
-    norms = jnp.concatenate([before_ref[0:2, :], *sums], axis=0)
+    norms = [before_ref[0:1, :], before_ref[1:2, :], *sums]
+    shape = (modes // 4, modes)
+    own = lax.broadcasted_iota(jnp.int32, shape, 1) // 4 == lax.broadcasted_iota(jnp.int32, shape, 0)
+    picked = jnp.concatenate([jnp.where(own, norm, 0.0) for norm in norms], axis=1)
+    shape = (4 * modes, LANES)
+    source = lax.broadcasted_iota(jnp.int32, shape, 0)
+    target = source // modes * 4 + source % 4
+    moves = jnp.where(lax.broadcasted_iota(jnp.int32, shape, 1) == target, 1.0, 0.0).astype(BF16)
+    high, low = split(picked)
+    rows = dot(high, moves) + dot(low, moves)
     for group in range(modes // 4):
-        out_ref[group * 12 : group * 12 + 8, :] = held_ref[group * 8 : group * 8 + 8, :]
-        out_ref[group * 12 + 8 : group * 12 + 12, :] = norms
-
-
-def regroup_kernel(group_ref, x_ref, out_ref):
-    norms = x_ref[8:12, :]
+        out_ref[group * 9 : group * 9 + 8, :] = held_ref[group * 8 : group * 8 + 8, :]
+        out_ref[group * 9 + 8 : group * 9 + 9, :] = rows[group : group + 1, :]
+
+
+def regroup_kernel(x_ref, out_ref):
+    norms = x_ref[8:9, :]
     for source in range(1, 32):
-        norms = norms + x_ref[source * 12 + 8 : source * 12 + 12, :]
-    norms = pltpu.roll(norms, (LANES - 4 * group_ref[0]) % LANES, 1)
-    lane = lax.broadcasted_iota(jnp.int32, (1, LANES), 1)
-    own = jnp.where(lane < 4, norms[0:1, :], 0.0)
-    for k in range(1, 4):
-        moved = pltpu.roll(norms[k : k + 1, :], 4 * k, 1)
-        own = jnp.where((lane >= 4 * k) & (lane < 4 * k + 4), moved, own)
+        norms = norms + x_ref[source * 9 + 8 : source * 9 + 9, :]
     for target in range(16):
         for half in range(2):
             source = target * 2 + half
             at = target * 17 + half * 8
-            out_ref[at : at + 8, :] = x_ref[source * 12 : source * 12 + 8, :]
-        out_ref[target * 17 + 16 : target * 17 + 17, :] = own
+            out_ref[at : at + 8, :] = x_ref[source * 9 : source * 9 + 8, :]
+        out_ref[target * 17 + 16 : target * 17 + 17, :] = norms
 
 
 def leave_kernel(x_ref, field_ref, errors_ref):
@@ -315,10 +323,7 @@
 
 def shards(field, beta, quartets, intersections):
     waves = jnp.asarray(host_waves())
-    field, group, th, tl = lax.optimization_barrier(
-        (field, *(lax.axis_index(a).astype(jnp.int32) for a in ("mode", "th", "tl")))
-    )
-    group, th, tl = (group[None], th[None], tl[None])
+    th, tl = (lax.axis_index(a).astype(jnp.int32)[None] for a in ("th", "tl"))
     weights = intersections.reshape(1, -1)
     along, across = (("th", "tl"), "mode")
     vmem = pl.BlockSpec(memory_space=pltpu.VMEM)
@@ -338,18 +343,26 @@
         return pl.pallas_call(
             spectral_kernel,
             out_shape=rows_of(256),
-            in_specs=[smem] * 3 + [vmem] * 2,
+            in_specs=[vmem] * 4,
             out_specs=vmem,
             compiler_params=limit,
-        )(th, tl, beta, state, waves)
-
+        )(state, rotor, small, waves)
+
+    square = jax.ShapeDtypeStruct((2, LANES, LANES), F32)
+    rotor, small = pl.pallas_call(
+        rotor_kernel,
+        out_shape=(square, square),
+        in_specs=[smem] * 3,
+        out_specs=(vmem, vmem),
+        compiler_params=limit,
+    )(th, tl, beta)
     state = pl.pallas_call(
         enter_kernel,
         out_shape=rows_of(256),
-        in_specs=[vmem],
+        in_specs=[vmem, vmem],
         out_specs=vmem,
         compiler_params=limit,
-    )(field)
+    )(field, small)
     state = exchange(state, along, 16)
     state = placed(first_radix_kernel, state, tl)
     state = exchange(state, "tl", 4)
@@ -362,7 +375,7 @@
         state = exchange(state, across, 32)
         out = pl.pallas_call(
             functools.partial(kerr_kernel, last),
-            out_shape=rows_of(384) if last else (rows_of(256), rows_of(8)),
+            out_shape=rows_of(288) if last else (rows_of(256), rows_of(8)),
             in_specs=[vmem] * (3 + len(norms)),
             out_specs=vmem if last else (vmem, vmem),
             scratch_shapes=[pltpu.VMEM((256, LANES), F32)] if last else [],
@@ -379,10 +392,10 @@
     state = pl.pallas_call(
         regroup_kernel,
         out_shape=rows_of(272),
-        in_specs=[smem, vmem],
+        in_specs=[vmem],
         out_specs=vmem,
         compiler_params=limit,
-    )(group, state)
+    )(state)
     state = exchange(state, along, 16)
     return pl.pallas_call(
         leave_kernel,

time: 173 us -> 172 us (level)
    pallas_call x6 -> x7, Pallas kernels: 8.05 us -> 7.43 us  [the longest x2 4.62 us: shards(): pl.pallas_call(functools.partial(kerr_kernel, last), out_shape=rows_of(28...]
where the time goes in v3:
time: 172 us; the launch traced here: 171 us
  blocking collectives  160 us (93%)
  Pallas kernels  8.49 us (5%)
    all_to_all x10, blocking collectives, exchange(): return lax.all_to_all(tiles, axes, 0, 0, tiled=True).reshape(array.shape)  160 us
    pallas_call x2, Pallas kernels, shards(): pl.pallas_call(functools.partial(kerr_kernel, last), out_shape=rows_of(28...  4.62 us

profile of v3, /device:TPU:32, one launch (start us, length us, event | category | flops | bytes accessed | tf_op | source)
XLA Modules:
  0.0 171.4 jit_solution(15497477593046694451)
XLA Ops:
  0.6 0.0 copy-start
  0.7 0.8 copy-done.4
  1.4 0.8 shard_map.68
  2.2 0.9 copy-done.1
  3.1 0.1 shard_map.69
  3.2 29.2 %all_to_all.50 = f32[16,2,8,128]{3,2,1,0:T(8,128)S(1)} all-to-all(f32[16,2,8,128]{3,2,1,0:T(8,128)S(1)} %bitcast.37), channel_id=1, replica_groups=mesh['mode'=32,'th'=4,'tl'=4] {'th','tl'}, dimensions={0} | all-to-all | bytes 262144 | tf_op jit(solution)/shard_map/all_to_all | solution.py:321
  32.4 0.1 shard_map.70
  32.6 8.8 %all_to_all.51 = f32[4,8,8,128]{3,2,1,0:T(8,128)S(1)} all-to-all(f32[4,8,8,128]{3,2,1,0:T(8,128)S(1)} %bitcast.43), channel_id=1, replica_groups=mesh['mode'=32,'th'=4,'tl'=4] {'tl'}, dimensions={0} | all-to-all | bytes 262144 | tf_op jit(solution)/shard_map/all_to_all | solution.py:321
  41.4 0.9 shard_map.71
  42.4 18.2 %all_to_all.52 = f32[16,2,8,128]{3,2,1,0:T(8,128)S(1)} all-to-all(f32[16,2,8,128]{3,2,1,0:T(8,128)S(1)} %bitcast.36), channel_id=1, replica_groups=mesh['mode'=32,'th'=4,'tl'=4] {'th','tl'}, dimensions={0} | all-to-all | bytes 262144 | tf_op jit(solution)/shard_map/all_to_all | solution.py:321
  60.5 0.1 shard_map.72
  60.6 14.9 %all_to_all.53 = f32[32,1,8,128]{3,2,1,0:T(8,128)S(1)} all-to-all(f32[32,1,8,128]{3,2,1,0:T(8,128)S(1)} %bitcast.45), channel_id=1, replica_groups=mesh['mode'=32,'th'=4,'tl'=4] {'mode'}, dimensions={0} | all-to-all | bytes 262144 | tf_op jit(solution)/shard_map/all_to_all | solution.py:321
  75.5 2.3 %shard_map.73 = (f32[256,128]{1,0:T(8,128)S(1)}, f32[8,128]{1,0:T(8,128)S(1)}) custom-call(f32[256,128]{1,0:T(8,128)S(1)} %bitcast.39, s32[4,1024]{1,0:T(4,128)S(1)} %copy-done.2, f32[1,1024]{1,0:T(1,128)S(1)} %bitcast.49), custom_call_target="tpu_custom_call" | custom-call | tf_op jit(solution)/shard_map/pallas_call | solution.py:376
  77.8 11.3 %all_to_all.54 = f32[32,1,8,128]{3,2,1,0:T(8,128)S(1)} all-to-all(f32[32,1,8,128]{3,2,1,0:T(8,128)S(1)} %bitcast.48), channel_id=1, replica_groups=mesh['mode'=32,'th'=4,'tl'=4] {'mode'}, dimensions={0} | all-to-all | bytes 262144 | tf_op jit(solution)/shard_map/all_to_all | solution.py:321
  89.1 0.1 shard_map.74
  89.1 18.1 %all_to_all.55 = f32[16,2,8,128]{3,2,1,0:T(8,128)S(1)} all-to-all(f32[16,2,8,128]{3,2,1,0:T(8,128)S(1)} %bitcast.47), channel_id=1, replica_groups=mesh['mode'=32,'th'=4,'tl'=4] {'th','tl'}, dimensions={0} | all-to-all | bytes 262144 | tf_op jit(solution)/shard_map/all_to_all | solution.py:321
  107.3 0.9 shard_map.75
  108.2 19.1 %all_to_all.56 = f32[16,2,8,128]{3,2,1,0:T(8,128)S(1)} all-to-all(f32[16,2,8,128]{3,2,1,0:T(8,128)S(1)} %bitcast.34), channel_id=1, replica_groups=mesh['mode'=32,'th'=4,'tl'=4] {'th','tl'}, dimensions={0} | all-to-all | bytes 262144 | tf_op jit(solution)/shard_map/all_to_all | solution.py:321
  127.4 0.1 shard_map.76
  127.4 11.2 %all_to_all.57 = f32[32,1,8,128]{3,2,1,0:T(8,128)S(1)} all-to-all(f32[32,1,8,128]{3,2,1,0:T(8,128)S(1)} %bitcast.41), channel_id=1, replica_groups=mesh['mode'=32,'th'=4,'tl'=4] {'mode'}, dimensions={0} | all-to-all | bytes 262144 | tf_op jit(solution)/shard_map/all_to_all | solution.py:321
  138.6 2.3 %shard_map.77 = f32[288,128]{1,0:T(8,128)S(1)} custom-call(f32[256,128]{1,0:T(8,128)S(1)} %bitcast.38, s32[4,1024]{1,0:T(4,128)S(1)} %copy-done.2, f32[1,1024]{1,0:T(1,128)S(1)} %bitcast.50, f32[8,128]{1,0:T(8,128)S(1)} %get-tuple-element.9.refs_0_), custom_call_target="tpu_custom_call" | custom-call | tf_op jit(solution)/shard_map/pallas_call | solution.py:376
  140.9 11.3 %all_to_all.58 = f32[32,9,1,128]{3,2,1,0:T(1,128)S(1)} all-to-all(f32[32,9,1,128]{3,2,1,0:T(1,128)S(1)} %bitcast.29), channel_id=1, replica_groups=mesh['mode'=32,'th'=4,'tl'=4] {'mode'}, dimensions={0} | all-to-all | bytes 294912 | tf_op jit(solution)/shard_map/all_to_all | solution.py:321
  152.3 18.3 %all_to_all.59 = f32[16,17,1,128]{3,2,1,0:T(1,128)S(1)} all-to-all(f32[16,17,1,128]{3,2,1,0:T(1,128)S(1)} %bitcast.32), channel_id=1, replica_groups=mesh['mode'=32,'th'=4,'tl'=4] {'th','tl'}, dimensions={0} | all-to-all | bytes 278528 | tf_op jit(solution)/shard_map/all_to_all | solution.py:321
  170.6 0.8 shard_map.79
  (8 shorter events, 0.1 us)
Async XLA Ops:
  0.6 40.8 %copy-start = (bf16[4,2,256,256]{3,2,1,0:T(8,128)(2,1)S(1)}, bf16[4,2,256,256]{3,2,1,0:T(8,128)(2,1)}, u32[]{:S(2)}) copy-start(bf16[4,2,256,256]{3,2,1,0:T(8,128)(2,1)} %constant.9.clone.waves_ref) | copy-start | bytes 3145732
  0.6 0.8 copy-start.4
  2.2 0.9 copy-start.1
  60.6 15.0 %copy-start.2 = (s32[4,1024]{1,0:T(4,128)S(1)}, s32[4,1024]{1,0:T(4,128)}, u32[]{:S(2)}) copy-start(s32[4,1024]{1,0:T(4,128)} %quartets_ref.3) | copy-start | bytes 49156
  60.6 14.9 %copy-start.3 = (f32[1024]{0:T(1024)S(1)}, f32[1024]{0:T(1024)}, u32[]{:S(2)}) copy-start(f32[1024]{0:T(1024)} %param.8) | copy-start | bytes 12292

commit v4 on v3

--- a/solution.py
+++ b/solution.py
@@ -13,6 +13,7 @@
 
 STEPS = 2
 LANES = 128
+HALF = 64
 TIME = 65536
 QUARTER = TIME // 4
 TILE = 256
@@ -34,13 +35,7 @@
     ahead = np.block([[wave.real, -wave.imag], [wave.imag, wave.real]])
     back = np.block([[wave.real, wave.imag], [-wave.imag, wave.real]])
 
-    def row_order(place):
-        return np.array([ri * LANES + p for p, ri in place])
-
-    tile_order = row_order(
-        [(v * 16 + w, ri) for w in range(16) for ri in range(2) for v in range(8)]
-    )
-    tables = (ahead[:, tile_order], ahead.T, back.T, back[tile_order] / TIME)
+    tables = (ahead, ahead.T, back.T, back / TIME)
     return np.stack([two_parts(table) for table in tables])
 
 
@@ -106,7 +101,7 @@
     return (lax.broadcasted_iota(jnp.int32, (8, LANES), axis) for axis in range(2))
 
 
-def rotor_kernel(th_ref, tl_ref, beta_ref, rotor_ref, small_ref):
+def rotor_kernel(yx_ref, c_ref, th_ref, tl_ref, beta_ref, rotor_ref, small_ref):
     offset, slope, curve = (beta_ref[k, th_ref[0]] for k in range(3))
     shape = (LANES, LANES)
     row, lane = (lax.broadcasted_iota(jnp.int32, shape, axis) for axis in range(2))
@@ -138,11 +133,6 @@
     return [(sr + tr, si + ti), (dr + ui, di - ur), (sr - tr, si - ti), (dr - ui, di + ur)]
 
 
-def radix_back(x):
-    out = radix_ahead(x)
-    return [out[0], out[3], out[2], out[1]]
-
-
 def turned_back(pair, c, s):
     re, im = pair
     return (re * c + im * s, im * c - re * s)
@@ -166,55 +156,96 @@
                     out_ref[pl.ds(first, 4, stride=16), :] = pair[ri][v0 * 4 : v0 * 4 + 4]
 
 
-def middle_twists(th_ref, tl_ref):
-    row, lane = row_and_lane()
-    place = row * 2048 + lane + (th_ref[0] * 4 + tl_ref[0]) * LANES
+def first_lanes(shape):
+    return lax.broadcasted_iota(jnp.int32, shape, len(shape) - 1) < HALF
+
+
+def swapped(array):
+    return pltpu.roll(array, HALF, 1)
+
+
+def times_i(array):
+    moved = swapped(array)
+    return jnp.where(first_lanes(array.shape), -moved, moved)
+
+
+def middle_twists(yx_ref, th_ref, tl_ref):
+    lane = lax.broadcasted_iota(jnp.int32, (1, LANES), 1)
+    yx, w = (yx_ref[0], th_ref[0] * 4 + tl_ref[0])
+    place = yx // 2 * 2048 + w * LANES + yx % 2 * HALF + lane % HALF
     return [None] + [twist(f * place) for f in range(1, 4)]
 
 
-def ahead_kernel(th_ref, tl_ref, x_ref, out_ref):
-    twists = middle_twists(th_ref, tl_ref)
-    for low in range(4):
-        y = radix_ahead(
-            [
-                tuple(x_ref[pl.ds(a * 64 + low * 2 + ri, 8, stride=8), :] for ri in range(2))
-                for a in range(4)
-            ]
-        )
-        for f in range(4):
-            re, im = turned_back(y[f], *twists[f]) if f else y[f]
-            at = low * 64 + f * 16
-            out_ref[at : at + 8, :] = re
-            out_ref[at + 8 : at + 16, :] = im
-
-
-def back_kernel(th_ref, tl_ref, x_ref, out_ref):
-    twists = middle_twists(th_ref, tl_ref)
-    for low in range(4):
-        y = []
-        for f in range(4):
-            at = low * 64 + f * 16
-            pair = (x_ref[at : at + 8, :], x_ref[at + 8 : at + 16, :])
-            y.append(turned(pair, *twists[f]) if f else pair)
-        for a, pair in enumerate(radix_back(y)):
-            for ri in range(2):
-                out_ref[pl.ds(a * 64 + low * 2 + ri, 8, stride=8), :] = pair[ri]
-
-
-def spectral_kernel(x_ref, rotor_ref, small_ref, waves_ref, out_ref):
+def back_kernel(yx_ref, c_ref, th_ref, tl_ref, x_ref, keep_ref, send_ref):
+    twists = middle_twists(yx_ref, th_ref, tl_ref)
+    y = [x_ref[pl.ds(f, HALF, stride=4), :] for f in range(4)]
+    for f in range(1, 4):
+        c, s = twists[f]
+        y[f] = y[f] * c + times_i(y[f]) * s
+    even, odd = (y[0] + y[2], y[1] + y[3])
+    less, turn = (y[0] - y[2], times_i(y[1] - y[3]))
+    x = [even + odd, less + turn, even - odd, less - turn]
+    first = c_ref[0] == 0
+    for low in range(2):
+        rows = slice(low * HALF, low * HALF + HALF)
+        keep_ref[rows, :] = jnp.where(first, x[low], x[low + 2])
+        send_ref[rows, :] = jnp.where(first, x[low + 2], x[low])
+
+
+def ahead_kernel(yx_ref, c_ref, th_ref, tl_ref, keep_ref, came_ref, out_ref):
+    twists = middle_twists(yx_ref, th_ref, tl_ref)
+    first = c_ref[0] == 0
+    kept = [keep_ref[low * HALF : low * HALF + HALF, :] for low in range(2)]
+    came = [came_ref[low * HALF : low * HALF + HALF, :] for low in range(2)]
+    x = [jnp.where(first, k, m) for k, m in zip(kept, came)]
+    x += [jnp.where(first, m, k) for k, m in zip(kept, came)]
+    even, odd = (x[0] + x[2], x[1] + x[3])
+    less, turn = (x[0] - x[2], times_i(x[1] - x[3]))
+    y = [even + odd, less - turn, even - odd, less + turn]
+    for f in range(4):
+        if f:
+            c, s = twists[f]
+            y[f] = y[f] * c - times_i(y[f]) * s
+        out_ref[pl.ds(f, HALF, stride=4), :] = y[f]
+
+
+def spectral_kernel(from_tiles, x_ref, rotor_ref, small_ref, waves_ref, out_ref, held_ref):
     rotor = (rotor_ref[0], rotor_ref[1])
     small = (small_ref[0], small_ref[1])
-    y = from_left(waves_ref, 0, x_ref[...])
+    first = first_lanes((LANES, LANES))
+    for tile in range(32):
+        if from_tiles:
+            w, ri = divmod(tile, 2)
+            held_ref[pl.ds(ri * LANES + w, 8, stride=16), :] = x_ref[tile * 8 : tile * 8 + 8, :]
+        elif tile < 16:
+            v, half = divmod(tile, 2)
+            at = half * LANES + v * 16
+            held_ref[at : at + 16, :] = x_ref[tile * 16 : tile * 16 + 16, :]
+    x = held_ref[...]
+    if not from_tiles:
+        low, high = (x[:LANES], x[LANES:])
+        x = jnp.concatenate(
+            [jnp.where(first, low, swapped(high)), jnp.where(first, swapped(low), high)], axis=0
+        )
+    y = from_left(waves_ref, 0, x)
     re, im = turned_back((y[:LANES], y[LANES:]), *small)
     y = from_right(jnp.concatenate([re, im], axis=1), waves_ref, 1)
     re, im = turned((y[:, :LANES], y[:, LANES:]), *rotor)
     y = from_right(jnp.concatenate([re, im], axis=1), waves_ref, 2)
     re, im = turned((y[:, :LANES], y[:, LANES:]), *small)
-    out_ref[...] = from_left(waves_ref, 3, jnp.concatenate([re, im], axis=0))
+    y = from_left(waves_ref, 3, jnp.concatenate([re, im], axis=0))
+    re, im = (y[:LANES], y[LANES:])
+    halves = (jnp.where(first, re, swapped(im)), jnp.where(first, swapped(re), im))
+    for v in range(8):
+        for half in range(2):
+            at = v * 32 + half * 16
+            out_ref[at : at + 16, :] = halves[half][v * 16 : v * 16 + 16]
 
 
 def one_hots(quartets_ref, modes):
-    ids = lax.broadcasted_iota(jnp.int32, (modes, quartets_ref.shape[1]), 0)
+    row = lax.broadcasted_iota(jnp.int32, (modes, 1), 0)
+    half = modes // 2
+    ids = row % half // 4 * 8 + row // half * 4 + row % 4
     return [
         jnp.where(quartets_ref[k : k + 1, :] == ids, 1.0, 0.0).astype(BF16) for k in range(4)
     ]
@@ -245,11 +276,16 @@
     return total
 
 
-def kerr_kernel(last, x_ref, quartets_ref, weights_ref, *refs):
-    modes = x_ref.shape[0] // 2
-    linear = jnp.concatenate(
-        [x_ref[pl.ds(ri, modes, stride=2), :].T for ri in range(2)], axis=0
-    )
+def kerr_kernel(last, c_ref, keep_ref, came_ref, quartets_ref, weights_ref, *refs):
+    modes = keep_ref.shape[0]
+    mine = c_ref[0] == 0
+    blocks = []
+    for low in range(2):
+        rows = slice(low * HALF, low * HALF + HALF)
+        kept, came = (keep_ref[rows, :], came_ref[rows, :])
+        both = [jnp.where(mine, kept, came), jnp.where(mine, came, kept)]
+        blocks.append(jnp.concatenate(both, axis=0).T)
+    linear = jnp.concatenate([y[:HALF] for y in blocks] + [y[HALF:] for y in blocks], axis=0)
     hot = one_hots(quartets_ref, modes)
     first = kerr_term(linear, hot, weights_ref)
     second = kerr_term(linear + first, hot, weights_ref)
@@ -257,9 +293,13 @@
     estimate = 0.5 * (second - first)
     sums = [jnp.sum(y * y, axis=0, keepdims=True) for y in (estimate, updated)]
     if not last:
-        out_ref, sums_ref = refs
-        for ri in range(2):
-            out_ref[pl.ds(ri, modes, stride=2), :] = updated[ri * LANES : (ri + 1) * LANES].T
+        kept_ref, send_ref, sums_ref = refs
+        for low in range(2):
+            rows = slice(low * HALF, low * HALF + HALF)
+            parts = [updated[ri * LANES + low * HALF :][:HALF] for ri in range(2)]
+            both = jnp.concatenate(parts, axis=0).T
+            kept_ref[rows, :] = jnp.where(mine, both[:HALF], both[HALF:])
+            send_ref[rows, :] = jnp.where(mine, both[HALF:], both[:HALF])
         sums_ref[0:1, :] = sums[0]
         sums_ref[1:2, :] = sums[1]
         return
@@ -276,20 +316,27 @@
     moves = jnp.where(lax.broadcasted_iota(jnp.int32, shape, 1) == target, 1.0, 0.0).astype(BF16)
     high, low = split(picked)
     rows = dot(high, moves) + dot(low, moves)
-    for group in range(modes // 4):
-        out_ref[group * 9 : group * 9 + 8, :] = held_ref[group * 8 : group * 8 + 8, :]
-        out_ref[group * 9 + 8 : group * 9 + 9, :] = rows[group : group + 1, :]
+    for block in range(modes // 4):
+        c, yx = divmod(block, 16)
+        at = (yx * 2 + c) * 9
+        out_ref[at : at + 8, :] = held_ref[block * 8 : block * 8 + 8, :]
+        out_ref[at + 8 : at + 9, :] = rows[block : block + 1, :]
 
 
 def regroup_kernel(x_ref, out_ref):
     norms = x_ref[8:9, :]
     for source in range(1, 32):
         norms = norms + x_ref[source * 9 + 8 : source * 9 + 9, :]
+    first = first_lanes((8, LANES))
+    for v in range(8):
+        for c in range(2):
+            at = [(v * 4 + half * 2 + c) * 9 for half in range(2)]
+            low, high = (x_ref[b : b + 8, :] for b in at)
+            made = (jnp.where(first, low, swapped(high)), jnp.where(first, swapped(low), high))
+            for a in range(2):
+                to = (c * 8 + a * 4 + v // 2) * 17 + v % 2 * 8
+                out_ref[to : to + 8, :] = made[a]
     for target in range(16):
-        for half in range(2):
-            source = target * 2 + half
-            at = target * 17 + half * 8
-            out_ref[at : at + 8, :] = x_ref[source * 9 : source * 9 + 8, :]
         out_ref[target * 17 + 16 : target * 17 + 17, :] = norms
 
 
@@ -323,28 +370,35 @@
 
 def shards(field, beta, quartets, intersections):
     waves = jnp.asarray(host_waves())
-    th, tl = (lax.axis_index(a).astype(jnp.int32)[None] for a in ("th", "tl"))
+    yx, c, th, tl = lax.optimization_barrier(
+        tuple(lax.axis_index(a).astype(jnp.int32)[None] for a in ("yx", "c", "th", "tl"))
+    )
     weights = intersections.reshape(1, -1)
-    along, across = (("th", "tl"), "mode")
+    along, across, chips = (("th", "tl"), ("yx", "c"), ("yx", "th", "tl"))
+    place = (yx, c, th, tl)
     vmem = pl.BlockSpec(memory_space=pltpu.VMEM)
     smem = pl.BlockSpec(memory_space=pltpu.SMEM)
     limit = pltpu.CompilerParams(vmem_limit_bytes=16 * 1024 * 1024)
 
-    def placed(kernel, state, *numbers):
+    def placed(kernel, numbers, arrays, results):
         return pl.pallas_call(
             kernel,
-            out_shape=rows_of(256),
-            in_specs=[smem] * len(numbers) + [vmem],
-            out_specs=vmem,
+            out_shape=results,
+            in_specs=[smem] * len(numbers) + [vmem] * len(arrays),
+            out_specs=tuple(vmem for _ in results) if isinstance(results, tuple) else vmem,
             compiler_params=limit,
-        )(*numbers, state)
-
-    def spectral(state):
+        )(*numbers, *arrays)
+
+    def other_core(array):
+        return lax.ppermute(array, "c", [(0, 1), (1, 0)])
+
+    def spectral(state, from_tiles):
         return pl.pallas_call(
-            spectral_kernel,
+            functools.partial(spectral_kernel, from_tiles),
             out_shape=rows_of(256),
             in_specs=[vmem] * 4,
             out_specs=vmem,
+            scratch_shapes=[pltpu.VMEM((256, LANES), F32)],
             compiler_params=limit,
         )(state, rotor, small, waves)
 
@@ -352,10 +406,10 @@
     rotor, small = pl.pallas_call(
         rotor_kernel,
         out_shape=(square, square),
-        in_specs=[smem] * 3,
+        in_specs=[smem] * 5,
         out_specs=(vmem, vmem),
         compiler_params=limit,
-    )(th, tl, beta)
+    )(*place, beta)
     state = pl.pallas_call(
         enter_kernel,
         out_shape=rows_of(256),
@@ -364,31 +418,31 @@
         compiler_params=limit,
     )(field, small)
     state = exchange(state, along, 16)
-    state = placed(first_radix_kernel, state, tl)
+    state = placed(first_radix_kernel, (tl,), (state,), rows_of(256))
     state = exchange(state, "tl", 4)
+    pair = (rows_of(128), rows_of(128))
     norms = []
     for step in range(STEPS):
         last = step == STEPS - 1
-        state = spectral(state)
-        state = exchange(state, along, 16)
-        state = placed(back_kernel, state, th, tl)
-        state = exchange(state, across, 32)
+        state = spectral(state, step == 0)
+        state = exchange(state, chips, 256)
+        keep, send = placed(back_kernel, place, (state,), pair)
+        came = other_core(send)
         out = pl.pallas_call(
             functools.partial(kerr_kernel, last),
-            out_shape=rows_of(288) if last else (rows_of(256), rows_of(8)),
-            in_specs=[vmem] * (3 + len(norms)),
-            out_specs=vmem if last else (vmem, vmem),
+            out_shape=rows_of(288) if last else (*pair, rows_of(8)),
+            in_specs=[smem] + [vmem] * (4 + len(norms)),
+            out_specs=vmem if last else (vmem, vmem, vmem),
             scratch_shapes=[pltpu.VMEM((256, LANES), F32)] if last else [],
             compiler_params=limit,
-        )(state, quartets, weights, *norms)
+        )(c, keep, came, quartets, weights, *norms)
         if last:
             state = exchange(out, across, 32)
             break
-        state, norm = out
+        keep, send, norm = out
         norms.append(norm)
-        state = exchange(state, across, 32)
-        state = placed(ahead_kernel, state, th, tl)
-        state = exchange(state, along, 16)
+        state = placed(ahead_kernel, place, (keep, other_core(send)), rows_of(256))
+        state = exchange(state, chips, 256)
     state = pl.pallas_call(
         regroup_kernel,
         out_shape=rows_of(272),
@@ -410,12 +464,12 @@
 
 
 def solution(mesh):
-    finer = Mesh(mesh.devices.reshape(-1, 4, 4), ("mode", "th", "tl"))
-    times = ("th", "tl")
+    finer = Mesh(mesh.devices.reshape(-1, 2, 4, 4), ("yx", "c", "th", "tl"))
+    modes, times = (("yx", "c"), ("th", "tl"))
     return jax.shard_map(
         shards,
         mesh=finer,
-        in_specs=(P(None, "mode", times), P(None, "mode"), P(), P()),
-        out_specs=(P(None, "mode", times), P(None, "mode")),
+        in_specs=(P(None, modes, times), P(None, modes), P(), P()),
+        out_specs=(P(None, modes, times), P(None, modes)),
         check_vma=False,
     )

time: 172 us -> 175 us (1.017)
  blocking collectives: 160 us -> 153 us
  starting transfers between devices: 0 us -> 5.91 us
  waiting for transfers between devices: 0 us -> 3.51 us
    all_to_all x10 -> x7, blocking collectives: 160 us -> 153 us  [exchange(): return lax.all_to_all(tiles, axes, 0, 0, tiled=True).reshape(array.shape)]
    ppermute x0 -> x3, starting transfers between devices: none -> 5.91 us  [other_core(): return lax.ppermute(array, 'c', [(0, 1), (1, 0)])]
    ppermute x0 -> x3, waiting for transfers between devices: none -> 3.51 us  [other_core(): return lax.ppermute(array, 'c', [(0, 1), (1, 0)])]
  transfers between devices with their start and end apart: 0 -> 3, of which waited for: 0 -> 3; matrix products, arithmetic and copies ran while one was open for 0% -> 0% of each run, Pallas kernels for 0% -> 0%
where the time goes in v4:
time: 175 us; the launch traced here: 174 us
  blocking collectives  153 us (87%)
  Pallas kernels  9.1 us (5%)
  starting transfers between devices  5.91 us (3%)
  waiting for transfers between devices  3.51 us (2%)
    all_to_all x7, blocking collectives, exchange(): return lax.all_to_all(tiles, axes, 0, 0, tiled=True).reshape(array.shape)  153 us
    ppermute x3, starting transfers between devices, other_core(): return lax.ppermute(array, 'c', [(0, 1), (1, 0)])  5.91 us
    pallas_call x2, Pallas kernels, shards(): pl.pallas_call(functools.partial(kerr_kernel, last), out_shape=rows_of(28...  4.58 us
    ppermute x3, waiting for transfers between devices, other_core(): return lax.ppermute(array, 'c', [(0, 1), (1, 0)])  3.51 us
  transfers between devices with their start and end apart: 3, of which 3 were waited for; matrix products, arithmetic and copies ran while one was open for 0% of the time, Pallas kernels for 0%

profile of v4, /device:TPU:32, one launch (start us, length us, event | category | flops | bytes accessed | tf_op | source)
XLA Modules:
  0.0 174.4 jit_solution(4744255425056475612)
XLA Ops:
  0.7 0.8 copy-done.4
  1.4 0.8 shard_map.68
  2.3 0.9 copy-done.1
  3.2 29.2 %all_to_all.35 = f32[16,2,8,128]{3,2,1,0:T(8,128)S(1)} all-to-all(f32[16,2,8,128]{3,2,1,0:T(8,128)S(1)} %bitcast.33), channel_id=1, replica_groups=mesh['yx'=16,'c'=2,'th'=4,'tl'=4] {'th','tl'}, dimensions={0} | all-to-all | bytes 262144 | tf_op jit(solution)/shard_map/all_to_all | solution.py:368
  32.6 8.8 %all_to_all.36 = f32[4,8,8,128]{3,2,1,0:T(8,128)S(1)} all-to-all(f32[4,8,8,128]{3,2,1,0:T(8,128)S(1)} %bitcast.38), channel_id=1, replica_groups=mesh['yx'=16,'c'=2,'th'=4,'tl'=4] {'tl'}, dimensions={0} | all-to-all | bytes 262144 | tf_op jit(solution)/shard_map/all_to_all | solution.py:368
  41.4 1.0 shard_map.71
  42.5 30.9 %all_to_all.37 = f32[256,1,1,128]{3,2,1,0:T(1,128)S(1)} all-to-all(f32[256,1,1,128]{3,2,1,0:T(1,128)S(1)} %bitcast.32), channel_id=1, replica_groups=mesh['yx'=16,'c'=2,'th'=4,'tl'=4] {'yx','th','tl'}, dimensions={0} | all-to-all | bytes 262144 | tf_op jit(solution)/shard_map/all_to_all | solution.py:368
  73.4 0.2 shard_map.72
  73.5 1.9 %collective-permute-start = (f32[128,128]{1,0:T(8,128)S(1)}, f32[128,128]{1,0:T(8,128)S(1)}, u32[]{:S(2)}, u32[]{:S(2)}) collective-permute-start(f32[128,128]{1,0:T(8,128)S(1)} %get-tuple-element.22), channel_id=1, source_target_pairs={{0,16},{16,0},{1,17},{17,1},{2,18},{18,2},{3,19},{19,3},{4,20},{20... | collective-permute-start | bytes 196616 | tf_op jit(solution)/shard_map/ppermute | solution.py:393
  75.5 1.2 collective-permute-done.came_ref
  76.7 2.3 %shard_map.73 = (f32[128,128]{1,0:T(8,128)S(1)}, f32[128,128]{1,0:T(8,128)S(1)}, f32[8,128]{1,0:T(8,128)S(1)}) custom-call(s32[1]{0:T(128)} %bitcast.1.c_ref, f32[128,128]{1,0:T(8,128)S(1)} %get-tuple-element.21.keep_ref, f32[128,128]{1,0:T(8,128)S(1)} %collective-permute-done.came_ref, s32[4,1024]{1,0:T(4,128)S(1)} %copy-done.2, f32[1,1024]{1,0:T(1,128)S(1)} %bitcast.39), custom_call_target="tpu_custom_call" | custom-call | tf_op jit(solution)/shard_map/pallas_call | solution.py:431
  79.0 2.1 %collective-permute-start.1 = (f32[128,128]{1,0:T(8,128)S(1)}, f32[128,128]{1,0:T(8,128)S(1)}, u32[]{:S(2)}, u32[]{:S(2)}) collective-permute-start(f32[128,128]{1,0:T(8,128)S(1)} %get-tuple-element.24), channel_id=1, source_target_pairs={{0,16},{16,0},{1,17},{17,1},{2,18},{18,2},{3,19},{19,3},{4,20},{20... | collective-permute-start | bytes 196616 | tf_op jit(solution)/shard_map/ppermute | solution.py:393
  81.0 1.1 collective-permute-done.1.came_ref
  82.1 0.2 shard_map.74
  82.3 27.9 %all_to_all.38 = f32[256,1,1,128]{3,2,1,0:T(1,128)S(1)} all-to-all(f32[256,1,1,128]{3,2,1,0:T(1,128)S(1)} %bitcast.36), channel_id=1, replica_groups=mesh['yx'=16,'c'=2,'th'=4,'tl'=4] {'yx','th','tl'}, dimensions={0} | all-to-all | bytes 262144 | tf_op jit(solution)/shard_map/all_to_all | solution.py:368
  110.1 1.1 shard_map.75
  111.2 26.5 %all_to_all.39 = f32[256,1,1,128]{3,2,1,0:T(1,128)S(1)} all-to-all(f32[256,1,1,128]{3,2,1,0:T(1,128)S(1)} %bitcast.30), channel_id=1, replica_groups=mesh['yx'=16,'c'=2,'th'=4,'tl'=4] {'yx','th','tl'}, dimensions={0} | all-to-all | bytes 262144 | tf_op jit(solution)/shard_map/all_to_all | solution.py:368
  137.7 0.2 shard_map.76
  137.9 1.9 %collective-permute-start.2 = (f32[128,128]{1,0:T(8,128)S(1)}, f32[128,128]{1,0:T(8,128)S(1)}, u32[]{:S(2)}, u32[]{:S(2)}) collective-permute-start(f32[128,128]{1,0:T(8,128)S(1)} %get-tuple-element.26), channel_id=1, source_target_pairs={{0,16},{16,0},{1,17},{17,1},{2,18},{18,2},{3,19},{19,3},{4,20},{20... | collective-permute-start | bytes 196616 | tf_op jit(solution)/shard_map/ppermute | solution.py:393
  139.8 1.2 collective-permute-done.2.came_ref
  141.0 2.3 %shard_map.77 = f32[288,128]{1,0:T(8,128)S(1)} custom-call(s32[1]{0:T(128)} %bitcast.1.c_ref, f32[128,128]{1,0:T(8,128)S(1)} %get-tuple-element.25.keep_ref, f32[128,128]{1,0:T(8,128)S(1)} %collective-permute-done.2.came_ref, s32[4,1024]{1,0:T(4,128)S(1)} %copy-done.2, f32[1,1024]{1,0:T(1,128)S(1)} %bitcast.40, f32[8,128]{1,0:T(8,128)S(1)} %get-tuple-element.27.refs_0_), custom_call_target="tpu_custom_call" | custom-call | tf_op jit(solution)/shard_map/pallas_call | solution.py:431
  143.4 11.6 %all_to_all.40 = f32[32,9,1,128]{3,2,1,0:T(1,128)S(1)} all-to-all(f32[32,9,1,128]{3,2,1,0:T(1,128)S(1)} %bitcast.25), channel_id=1, replica_groups=mesh['yx'=16,'c'=2,'th'=4,'tl'=4] {'yx','c'}, dimensions={0} | all-to-all | bytes 294912 | tf_op jit(solution)/shard_map/all_to_all | solution.py:368
  155.1 18.6 %all_to_all.41 = f32[16,17,1,128]{3,2,1,0:T(1,128)S(1)} all-to-all(f32[16,17,1,128]{3,2,1,0:T(1,128)S(1)} %bitcast.28), channel_id=1, replica_groups=mesh['yx'=16,'c'=2,'th'=4,'tl'=4] {'th','tl'}, dimensions={0} | all-to-all | bytes 278528 | tf_op jit(solution)/shard_map/all_to_all | solution.py:368
  173.6 0.8 shard_map.79
  (11 shorter events, 0.3 us)
Async XLA Ops:
  0.6 40.8 %copy-start = (bf16[4,2,256,256]{3,2,1,0:T(8,128)(2,1)S(1)}, bf16[4,2,256,256]{3,2,1,0:T(8,128)(2,1)}, u32[]{:S(2)}) copy-start(bf16[4,2,256,256]{3,2,1,0:T(8,128)(2,1)} %constant.20.clone.waves_ref) | copy-start | bytes 3145732
  0.7 0.8 copy-start.4
  2.2 0.9 copy-start.1
  73.4 3.3 %copy-start.2 = (s32[4,1024]{1,0:T(4,128)S(1)}, s32[4,1024]{1,0:T(4,128)}, u32[]{:S(2)}) copy-start(s32[4,1024]{1,0:T(4,128)} %quartets_ref.3) | copy-start | bytes 49156
  73.5 3.2 %copy-start.3 = (f32[1024]{0:T(1024)S(1)}, f32[1024]{0:T(1024)}, u32[]{:S(2)}) copy-start(f32[1024]{0:T(1024)} %param.8) | copy-start | bytes 12292
  73.5 3.1 %collective-permute-start = (f32[128,128]{1,0:T(8,128)S(1)}, f32[128,128]{1,0:T(8,128)S(1)}, u32[]{:S(2)}, u32[]{:S(2)}) collective-permute-start(f32[128,128]{1,0:T(8,128)S(1)} %get-tuple-element.22), channel_id=1, source_target_pairs={{0,16},{16,0},{1,17},{17,1},{2,18},{18,2},{3,19},{19,3},{4,20},{20... | collective-permute-start | bytes 196616 | tf_op jit(solution)/shard_map/ppermute | solution.py:393
  79.0 3.1 %collective-permute-start.1 = (f32[128,128]{1,0:T(8,128)S(1)}, f32[128,128]{1,0:T(8,128)S(1)}, u32[]{:S(2)}, u32[]{:S(2)}) collective-permute-start(f32[128,128]{1,0:T(8,128)S(1)} %get-tuple-element.24), channel_id=1, source_target_pairs={{0,16},{16,0},{1,17},{17,1},{2,18},{18,2},{3,19},{19,3},{4,20},{20... | collective-permute-start | bytes 196616 | tf_op jit(solution)/shard_map/ppermute | solution.py:393
  137.9 3.1 %collective-permute-start.2 = (f32[128,128]{1,0:T(8,128)S(1)}, f32[128,128]{1,0:T(8,128)S(1)}, u32[]{:S(2)}, u32[]{:S(2)}) collective-permute-start(f32[128,128]{1,0:T(8,128)S(1)} %get-tuple-element.26), channel_id=1, source_target_pairs={{0,16},{16,0},{1,17},{17,1},{2,18},{18,2},{3,19},{19,3},{4,20},{20... | collective-permute-start | bytes 196616 | tf_op jit(solution)/shard_map/ppermute | solution.py:393

commit v5 on v3

--- a/solution.py
+++ b/solution.py
@@ -97,8 +97,8 @@
 
 
 def twist(number):
-    turns = (number + TIME // 8) // QUARTER
-    rest = (number - turns * QUARTER).astype(F32)
+    turns = (number + TIME // 8) >> 14
+    rest = (number - (turns << 14)).astype(F32)
     return in_quarter(turns, *small_cosine_and_sine(rest * (2.0 * math.pi / TIME)))
 
 
@@ -106,11 +106,14 @@
     return (lax.broadcasted_iota(jnp.int32, (8, LANES), axis) for axis in range(2))
 
 
-def rotor_kernel(th_ref, tl_ref, beta_ref, rotor_ref, small_ref):
+def small_kernel(th_ref, small_ref):
+    row, lane = (lax.broadcasted_iota(jnp.int32, (LANES, LANES), axis) for axis in range(2))
+    small_ref[0], small_ref[1] = twist(4 * row * lane)
+
+
+def rotor_kernel(th_ref, tl_ref, beta_ref, after_ref, rotor_ref):
     offset, slope, curve = (beta_ref[k, th_ref[0]] for k in range(3))
-    shape = (LANES, LANES)
-    row, lane = (lax.broadcasted_iota(jnp.int32, shape, axis) for axis in range(2))
-    small_ref[0], small_ref[1] = twist(4 * row * lane)
+    row, lane = (lax.broadcasted_iota(jnp.int32, (LANES, LANES), axis) for axis in range(2))
     wave = 4 * (row + LANES * lane) + tl_ref[0]
     signed = jnp.where(wave < TIME // 2, wave, wave - TIME)
     frequency = signed.astype(F32) * (1.0 / (TIME / 2))
@@ -349,20 +352,30 @@
         )(state, rotor, small, waves)
 
     square = jax.ShapeDtypeStruct((2, LANES, LANES), F32)
-    rotor, small = pl.pallas_call(
+    cost = pl.CostEstimate(flops=4 * 10**8, bytes_accessed=2 * TIME, transcendentals=0)
+    small = pl.pallas_call(
+        small_kernel,
+        out_shape=square,
+        in_specs=[smem],
+        out_specs=vmem,
+        compiler_params=limit,
+        cost_estimate=cost,
+    )(th)
+    rotor = pl.pallas_call(
         rotor_kernel,
-        out_shape=(square, square),
-        in_specs=[smem] * 3,
-        out_specs=(vmem, vmem),
+        out_shape=square,
+        in_specs=[smem] * 3 + [vmem],
+        out_specs=vmem,
         compiler_params=limit,
-    )(th, tl, beta)
+        cost_estimate=cost,
+    )(th, tl, beta, small)
     state = pl.pallas_call(
         enter_kernel,
         out_shape=rows_of(256),
         in_specs=[vmem, vmem],
         out_specs=vmem,
         compiler_params=limit,
-    )(field, small)
+    )(field, rotor)
     state = exchange(state, along, 16)
     state = placed(first_radix_kernel, state, tl)
     state = exchange(state, "tl", 4)

time: 172 us -> 171 us (level)
  no operation moved by 1% of the time
where the time goes in v5:
time: 171 us; the launch traced here: 170 us
  blocking collectives  161 us (94%)
  Pallas kernels  8.38 us (5%)
    all_to_all x10, blocking collectives, exchange(): return lax.all_to_all(tiles, axes, 0, 0, tiled=True).reshape(array.shape)  161 us
    pallas_call x2, Pallas kernels, shards(): pl.pallas_call(functools.partial(kerr_kernel, last), out_shape=rows_of(28...  4.61 us

profile of v5, /device:TPU:32, one launch (start us, length us, event | category | flops | bytes accessed | tf_op | source)
XLA Modules:
  0.0 170.4 jit_solution(8934454759284025692)
XLA Ops:
  0.6 0.1 shard_map.68.after_ref.small_ref
  0.7 0.6 copy-done.4
  1.3 0.7 shard_map.69.after_ref.rotor_ref
  2.0 0.2 copy-done.1
  2.2 0.1 shard_map.70
  2.3 29.2 %all_to_all.50 = f32[16,2,8,128]{3,2,1,0:T(8,128)S(1)} all-to-all(f32[16,2,8,128]{3,2,1,0:T(8,128)S(1)} %bitcast.37), channel_id=1, replica_groups=mesh['mode'=32,'th'=4,'tl'=4] {'th','tl'}, dimensions={0} | all-to-all | bytes 262144 | tf_op jit(solution)/shard_map/all_to_all | solution.py:324
  31.5 0.1 shard_map.71
  31.6 8.8 %all_to_all.51 = f32[4,8,8,128]{3,2,1,0:T(8,128)S(1)} all-to-all(f32[4,8,8,128]{3,2,1,0:T(8,128)S(1)} %bitcast.43), channel_id=1, replica_groups=mesh['mode'=32,'th'=4,'tl'=4] {'tl'}, dimensions={0} | all-to-all | bytes 262144 | tf_op jit(solution)/shard_map/all_to_all | solution.py:324
  40.5 0.9 shard_map.72
  41.4 18.2 %all_to_all.52 = f32[16,2,8,128]{3,2,1,0:T(8,128)S(1)} all-to-all(f32[16,2,8,128]{3,2,1,0:T(8,128)S(1)} %bitcast.36), channel_id=1, replica_groups=mesh['mode'=32,'th'=4,'tl'=4] {'th','tl'}, dimensions={0} | all-to-all | bytes 262144 | tf_op jit(solution)/shard_map/all_to_all | solution.py:324
  59.6 0.1 shard_map.73
  59.6 0.0 copy-start.2
  59.7 14.9 %all_to_all.53 = f32[32,1,8,128]{3,2,1,0:T(8,128)S(1)} all-to-all(f32[32,1,8,128]{3,2,1,0:T(8,128)S(1)} %bitcast.45), channel_id=1, replica_groups=mesh['mode'=32,'th'=4,'tl'=4] {'mode'}, dimensions={0} | all-to-all | bytes 262144 | tf_op jit(solution)/shard_map/all_to_all | solution.py:324
  74.6 2.3 %shard_map.74 = (f32[256,128]{1,0:T(8,128)S(1)}, f32[8,128]{1,0:T(8,128)S(1)}) custom-call(f32[256,128]{1,0:T(8,128)S(1)} %bitcast.39, s32[4,1024]{1,0:T(4,128)S(1)} %copy-done.2, f32[1,1024]{1,0:T(1,128)S(1)} %bitcast.49), custom_call_target="tpu_custom_call" | custom-call | tf_op jit(solution)/shard_map/pallas_call | solution.py:389
  76.9 11.3 %all_to_all.54 = f32[32,1,8,128]{3,2,1,0:T(8,128)S(1)} all-to-all(f32[32,1,8,128]{3,2,1,0:T(8,128)S(1)} %bitcast.48), channel_id=1, replica_groups=mesh['mode'=32,'th'=4,'tl'=4] {'mode'}, dimensions={0} | all-to-all | bytes 262144 | tf_op jit(solution)/shard_map/all_to_all | solution.py:324
  88.2 18.1 %all_to_all.55 = f32[16,2,8,128]{3,2,1,0:T(8,128)S(1)} all-to-all(f32[16,2,8,128]{3,2,1,0:T(8,128)S(1)} %bitcast.47), channel_id=1, replica_groups=mesh['mode'=32,'th'=4,'tl'=4] {'th','tl'}, dimensions={0} | all-to-all | bytes 262144 | tf_op jit(solution)/shard_map/all_to_all | solution.py:324
  106.3 0.9 shard_map.76
  107.2 19.1 %all_to_all.56 = f32[16,2,8,128]{3,2,1,0:T(8,128)S(1)} all-to-all(f32[16,2,8,128]{3,2,1,0:T(8,128)S(1)} %bitcast.34), channel_id=1, replica_groups=mesh['mode'=32,'th'=4,'tl'=4] {'th','tl'}, dimensions={0} | all-to-all | bytes 262144 | tf_op jit(solution)/shard_map/all_to_all | solution.py:324
  126.4 0.1 shard_map.77
  126.4 11.2 %all_to_all.57 = f32[32,1,8,128]{3,2,1,0:T(8,128)S(1)} all-to-all(f32[32,1,8,128]{3,2,1,0:T(8,128)S(1)} %bitcast.41), channel_id=1, replica_groups=mesh['mode'=32,'th'=4,'tl'=4] {'mode'}, dimensions={0} | all-to-all | bytes 262144 | tf_op jit(solution)/shard_map/all_to_all | solution.py:324
  137.6 2.3 %shard_map.78 = f32[288,128]{1,0:T(8,128)S(1)} custom-call(f32[256,128]{1,0:T(8,128)S(1)} %bitcast.38, s32[4,1024]{1,0:T(4,128)S(1)} %copy-done.2, f32[1,1024]{1,0:T(1,128)S(1)} %bitcast.50, f32[8,128]{1,0:T(8,128)S(1)} %get-tuple-element.5.refs_0_), custom_call_target="tpu_custom_call" | custom-call | tf_op jit(solution)/shard_map/pallas_call | solution.py:389
  139.9 11.4 %all_to_all.58 = f32[32,9,1,128]{3,2,1,0:T(1,128)S(1)} all-to-all(f32[32,9,1,128]{3,2,1,0:T(1,128)S(1)} %bitcast.29), channel_id=1, replica_groups=mesh['mode'=32,'th'=4,'tl'=4] {'mode'}, dimensions={0} | all-to-all | bytes 294912 | tf_op jit(solution)/shard_map/all_to_all | solution.py:324
  151.3 18.3 %all_to_all.59 = f32[16,17,1,128]{3,2,1,0:T(1,128)S(1)} all-to-all(f32[16,17,1,128]{3,2,1,0:T(1,128)S(1)} %bitcast.32), channel_id=1, replica_groups=mesh['mode'=32,'th'=4,'tl'=4] {'th','tl'}, dimensions={0} | all-to-all | bytes 278528 | tf_op jit(solution)/shard_map/all_to_all | solution.py:324
  169.6 0.8 shard_map.80
  (9 shorter events, 0.1 us)
Async XLA Ops:
  0.6 0.7 copy-start.4
  1.3 0.9 copy-start.1
  1.3 39.2 %copy-start = (bf16[4,2,256,256]{3,2,1,0:T(8,128)(2,1)S(1)}, bf16[4,2,256,256]{3,2,1,0:T(8,128)(2,1)}, u32[]{:S(2)}) copy-start(bf16[4,2,256,256]{3,2,1,0:T(8,128)(2,1)} %constant.9.clone.waves_ref) | copy-start | bytes 3145732
  59.6 14.9 %copy-start.2 = (s32[4,1024]{1,0:T(4,128)S(1)}, s32[4,1024]{1,0:T(4,128)}, u32[]{:S(2)}) copy-start(s32[4,1024]{1,0:T(4,128)} %quartets_ref.3) | copy-start | bytes 49156
  59.6 14.9 %copy-start.3 = (f32[1024]{0:T(1024)S(1)}, f32[1024]{0:T(1024)}, u32[]{:S(2)}) copy-start(f32[1024]{0:T(1024)} %param.8) | copy-start | bytes 12292

commit v6 on v5

--- a/solution.py
+++ b/solution.py
@@ -112,7 +112,9 @@
 
 
 def rotor_kernel(th_ref, tl_ref, beta_ref, after_ref, rotor_ref):
-    offset, slope, curve = (beta_ref[k, th_ref[0]] for k in range(3))
+    own = lax.broadcasted_iota(jnp.int32, beta_ref.shape, 1) == th_ref[0]
+    beta = jnp.sum(jnp.where(own, beta_ref[...], 0.0), axis=1, keepdims=True)
+    offset, slope, curve = (beta[k : k + 1, :] for k in range(3))
     row, lane = (lax.broadcasted_iota(jnp.int32, (LANES, LANES), axis) for axis in range(2))
     wave = 4 * (row + LANES * lane) + tl_ref[0]
     signed = jnp.where(wave < TIME // 2, wave, wave - TIME)
@@ -352,22 +354,21 @@
         )(state, rotor, small, waves)
 
     square = jax.ShapeDtypeStruct((2, LANES, LANES), F32)
-    cost = pl.CostEstimate(flops=4 * 10**8, bytes_accessed=2 * TIME, transcendentals=0)
     small = pl.pallas_call(
         small_kernel,
         out_shape=square,
         in_specs=[smem],
         out_specs=vmem,
         compiler_params=limit,
-        cost_estimate=cost,
+        cost_estimate=pl.CostEstimate(flops=10**9, bytes_accessed=2 * TIME, transcendentals=0),
     )(th)
     rotor = pl.pallas_call(
         rotor_kernel,
         out_shape=square,
-        in_specs=[smem] * 3 + [vmem],
+        in_specs=[smem] * 2 + [vmem] * 2,
         out_specs=vmem,
         compiler_params=limit,
-        cost_estimate=cost,
+        cost_estimate=pl.CostEstimate(flops=10**8, bytes_accessed=2 * TIME, transcendentals=0),
     )(th, tl, beta, small)
     state = pl.pallas_call(
         enter_kernel,

time: 171 us -> 170 us (level)
  no operation moved by 1% of the time
where the time goes in v6:
time: 170 us
  blocking collectives  160 us (94%)
  Pallas kernels  7.88 us (5%)
    all_to_all x10, blocking collectives, exchange(): return lax.all_to_all(tiles, axes, 0, 0, tiled=True).reshape(array.shape)  160 us
    pallas_call x2, Pallas kernels, shards(): pl.pallas_call(functools.partial(kerr_kernel, last), out_shape=rows_of(28...  4.6 us

profile of v6, /device:TPU:32, one launch (start us, length us, event | category | flops | bytes accessed | tf_op | source)
XLA Modules:
  0.0 169.7 jit_solution(8306785662857917608)
XLA Ops:
  0.7 0.1 shard_map.68.after_ref.small_ref
  0.7 0.0 copy-start
  0.8 0.6 copy-done.4
  1.3 0.2 shard_map.69.after_ref.rotor_ref
  1.5 0.0 copy-done.1
  1.6 0.1 shard_map.70
  1.6 29.2 %all_to_all.50 = f32[16,2,8,128]{3,2,1,0:T(8,128)S(1)} all-to-all(f32[16,2,8,128]{3,2,1,0:T(8,128)S(1)} %bitcast.37), channel_id=1, replica_groups=mesh['mode'=32,'th'=4,'tl'=4] {'th','tl'}, dimensions={0} | all-to-all | bytes 262144 | tf_op jit(solution)/shard_map/all_to_all | solution.py:326
  30.9 0.1 shard_map.71
  31.0 8.8 %all_to_all.51 = f32[4,8,8,128]{3,2,1,0:T(8,128)S(1)} all-to-all(f32[4,8,8,128]{3,2,1,0:T(8,128)S(1)} %bitcast.43), channel_id=1, replica_groups=mesh['mode'=32,'th'=4,'tl'=4] {'tl'}, dimensions={0} | all-to-all | bytes 262144 | tf_op jit(solution)/shard_map/all_to_all | solution.py:326
  39.8 0.9 shard_map.72
  40.8 18.2 %all_to_all.52 = f32[16,2,8,128]{3,2,1,0:T(8,128)S(1)} all-to-all(f32[16,2,8,128]{3,2,1,0:T(8,128)S(1)} %bitcast.36), channel_id=1, replica_groups=mesh['mode'=32,'th'=4,'tl'=4] {'th','tl'}, dimensions={0} | all-to-all | bytes 262144 | tf_op jit(solution)/shard_map/all_to_all | solution.py:326
  58.9 0.1 shard_map.73
  59.0 14.9 %all_to_all.53 = f32[32,1,8,128]{3,2,1,0:T(8,128)S(1)} all-to-all(f32[32,1,8,128]{3,2,1,0:T(8,128)S(1)} %bitcast.45), channel_id=1, replica_groups=mesh['mode'=32,'th'=4,'tl'=4] {'mode'}, dimensions={0} | all-to-all | bytes 262144 | tf_op jit(solution)/shard_map/all_to_all | solution.py:326
  73.9 2.3 %shard_map.74 = (f32[256,128]{1,0:T(8,128)S(1)}, f32[8,128]{1,0:T(8,128)S(1)}) custom-call(f32[256,128]{1,0:T(8,128)S(1)} %bitcast.39, s32[4,1024]{1,0:T(4,128)S(1)} %copy-done.2, f32[1,1024]{1,0:T(1,128)S(1)} %bitcast.49), custom_call_target="tpu_custom_call" | custom-call | tf_op jit(solution)/shard_map/pallas_call | solution.py:390
  76.2 11.3 %all_to_all.54 = f32[32,1,8,128]{3,2,1,0:T(8,128)S(1)} all-to-all(f32[32,1,8,128]{3,2,1,0:T(8,128)S(1)} %bitcast.48), channel_id=1, replica_groups=mesh['mode'=32,'th'=4,'tl'=4] {'mode'}, dimensions={0} | all-to-all | bytes 262144 | tf_op jit(solution)/shard_map/all_to_all | solution.py:326
  87.5 18.1 %all_to_all.55 = f32[16,2,8,128]{3,2,1,0:T(8,128)S(1)} all-to-all(f32[16,2,8,128]{3,2,1,0:T(8,128)S(1)} %bitcast.47), channel_id=1, replica_groups=mesh['mode'=32,'th'=4,'tl'=4] {'th','tl'}, dimensions={0} | all-to-all | bytes 262144 | tf_op jit(solution)/shard_map/all_to_all | solution.py:326
  105.6 0.9 shard_map.76
  106.6 19.1 %all_to_all.56 = f32[16,2,8,128]{3,2,1,0:T(8,128)S(1)} all-to-all(f32[16,2,8,128]{3,2,1,0:T(8,128)S(1)} %bitcast.34), channel_id=1, replica_groups=mesh['mode'=32,'th'=4,'tl'=4] {'th','tl'}, dimensions={0} | all-to-all | bytes 262144 | tf_op jit(solution)/shard_map/all_to_all | solution.py:326
  125.7 0.1 shard_map.77
  125.8 11.1 %all_to_all.57 = f32[32,1,8,128]{3,2,1,0:T(8,128)S(1)} all-to-all(f32[32,1,8,128]{3,2,1,0:T(8,128)S(1)} %bitcast.41), channel_id=1, replica_groups=mesh['mode'=32,'th'=4,'tl'=4] {'mode'}, dimensions={0} | all-to-all | bytes 262144 | tf_op jit(solution)/shard_map/all_to_all | solution.py:326
  136.9 2.3 %shard_map.78 = f32[288,128]{1,0:T(8,128)S(1)} custom-call(f32[256,128]{1,0:T(8,128)S(1)} %bitcast.38, s32[4,1024]{1,0:T(4,128)S(1)} %copy-done.2, f32[1,1024]{1,0:T(1,128)S(1)} %bitcast.50, f32[8,128]{1,0:T(8,128)S(1)} %get-tuple-element.5.refs_0_), custom_call_target="tpu_custom_call" | custom-call | tf_op jit(solution)/shard_map/pallas_call | solution.py:390
  139.2 11.4 %all_to_all.58 = f32[32,9,1,128]{3,2,1,0:T(1,128)S(1)} all-to-all(f32[32,9,1,128]{3,2,1,0:T(1,128)S(1)} %bitcast.29), channel_id=1, replica_groups=mesh['mode'=32,'th'=4,'tl'=4] {'mode'}, dimensions={0} | all-to-all | bytes 294912 | tf_op jit(solution)/shard_map/all_to_all | solution.py:326
  150.6 18.3 %all_to_all.59 = f32[16,17,1,128]{3,2,1,0:T(1,128)S(1)} all-to-all(f32[16,17,1,128]{3,2,1,0:T(1,128)S(1)} %bitcast.32), channel_id=1, replica_groups=mesh['mode'=32,'th'=4,'tl'=4] {'th','tl'}, dimensions={0} | all-to-all | bytes 278528 | tf_op jit(solution)/shard_map/all_to_all | solution.py:326
  169.0 0.8 shard_map.80
  (9 shorter events, 0.1 us)
Async XLA Ops:
  0.6 0.7 copy-start.4
  0.6 0.9 copy-start.1
  0.7 39.1 %copy-start = (bf16[4,2,256,256]{3,2,1,0:T(8,128)(2,1)S(1)}, bf16[4,2,256,256]{3,2,1,0:T(8,128)(2,1)}, u32[]{:S(2)}) copy-start(bf16[4,2,256,256]{3,2,1,0:T(8,128)(2,1)} %constant.9.clone.waves_ref) | copy-start | bytes 3145732
  59.0 14.9 %copy-start.2 = (s32[4,1024]{1,0:T(4,128)S(1)}, s32[4,1024]{1,0:T(4,128)}, u32[]{:S(2)}) copy-start(s32[4,1024]{1,0:T(4,128)} %quartets_ref.3) | copy-start | bytes 49156
  59.0 14.9 %copy-start.3 = (f32[1024]{0:T(1024)S(1)}, f32[1024]{0:T(1024)}, u32[]{:S(2)}) copy-start(f32[1024]{0:T(1024)} %param.8) | copy-start | bytes 12292

commit v7 on v6

--- a/solution.py
+++ b/solution.py
@@ -219,7 +219,9 @@
 
 
 def one_hots(quartets_ref, modes):
-    ids = lax.broadcasted_iota(jnp.int32, (modes, quartets_ref.shape[1]), 0)
+    row = lax.broadcasted_iota(jnp.int32, (modes, 1), 0)
+    x, core, y, low = (row >> 5, (row >> 4) & 1, (row >> 2) & 3, row & 3)
+    ids = ((y * 4 + x) * 2 + core) * 4 + low
     return [
         jnp.where(quartets_ref[k : k + 1, :] == ids, 1.0, 0.0).astype(BF16) for k in range(4)
     ]
@@ -330,7 +332,7 @@
     waves = jnp.asarray(host_waves())
     th, tl = (lax.axis_index(a).astype(jnp.int32)[None] for a in ("th", "tl"))
     weights = intersections.reshape(1, -1)
-    along, across = (("th", "tl"), "mode")
+    along, across = (("th", "tl"), ("x", "core", "y"))
     vmem = pl.BlockSpec(memory_space=pltpu.VMEM)
     smem = pl.BlockSpec(memory_space=pltpu.SMEM)
     limit = pltpu.CompilerParams(vmem_limit_bytes=16 * 1024 * 1024)
@@ -424,12 +426,12 @@
 
 
 def solution(mesh):
-    finer = Mesh(mesh.devices.reshape(-1, 4, 4), ("mode", "th", "tl"))
-    times = ("th", "tl")
+    finer = Mesh(mesh.devices.reshape(4, 4, 2, 4, 4), ("y", "x", "core", "th", "tl"))
+    modes, times = (("y", "x", "core"), ("th", "tl"))
     return jax.shard_map(
         shards,
         mesh=finer,
-        in_specs=(P(None, "mode", times), P(None, "mode"), P(), P()),
-        out_specs=(P(None, "mode", times), P(None, "mode")),
+        in_specs=(P(None, modes, times), P(None, modes), P(), P()),
+        out_specs=(P(None, modes, times), P(None, modes)),
         check_vma=False,
     )

time: 170 us -> 170 us (level)
  the two profiles are of different devices: /device:TPU:32 before, /device:TPU:2 now
where the time goes in v7:
time: 170 us; the launch traced here: 169 us
  blocking collectives  160 us (94%)
  Pallas kernels  7.86 us (5%)
    all_to_all x10, blocking collectives, exchange(): return lax.all_to_all(tiles, axes, 0, 0, tiled=True).reshape(array.shape)  160 us
    pallas_call x2, Pallas kernels, shards(): pl.pallas_call(functools.partial(kerr_kernel, last), out_shape=rows_of(28...  4.58 us

profile of v7, /device:TPU:2, one launch (start us, length us, event | category | flops | bytes accessed | tf_op | source)
XLA Modules:
  0.0 169.3 jit_solution(2363364442150735326)
XLA Ops:
  0.7 0.1 shard_map.68.after_ref.small_ref
  0.7 0.0 copy-start
  0.8 0.6 copy-done.4
  1.3 0.2 shard_map.69.after_ref.rotor_ref
  1.5 0.0 copy-done.1
  1.6 0.1 shard_map.70
  1.6 29.7 %all_to_all.50 = f32[16,2,8,128]{3,2,1,0:T(8,128)S(1)} all-to-all(f32[16,2,8,128]{3,2,1,0:T(8,128)S(1)} %bitcast.37), channel_id=1, replica_groups=mesh['y'=4,'x'=4,'core'=2,'th'=4,'tl'=4] {'th','tl'}, dimensions={0} | all-to-all | bytes 262144 | tf_op jit(solution)/shard_map/all_to_all | solution.py:328
  31.3 0.1 shard_map.71
  31.4 9.0 %all_to_all.51 = f32[4,8,8,128]{3,2,1,0:T(8,128)S(1)} all-to-all(f32[4,8,8,128]{3,2,1,0:T(8,128)S(1)} %bitcast.43), channel_id=1, replica_groups=mesh['y'=4,'x'=4,'core'=2,'th'=4,'tl'=4] {'tl'}, dimensions={0} | all-to-all | bytes 262144 | tf_op jit(solution)/shard_map/all_to_all | solution.py:328
  40.5 0.9 shard_map.72
  41.4 18.0 %all_to_all.52 = f32[16,2,8,128]{3,2,1,0:T(8,128)S(1)} all-to-all(f32[16,2,8,128]{3,2,1,0:T(8,128)S(1)} %bitcast.36), channel_id=1, replica_groups=mesh['y'=4,'x'=4,'core'=2,'th'=4,'tl'=4] {'th','tl'}, dimensions={0} | all-to-all | bytes 262144 | tf_op jit(solution)/shard_map/all_to_all | solution.py:328
  59.4 0.1 shard_map.73
  59.5 14.0 %all_to_all.53 = f32[32,1,8,128]{3,2,1,0:T(8,128)S(1)} all-to-all(f32[32,1,8,128]{3,2,1,0:T(8,128)S(1)} %bitcast.45), channel_id=1, replica_groups=mesh['y'=4,'x'=4,'core'=2,'th'=4,'tl'=4] {'x','core','y'}, dimensions={0} | all-to-all | bytes 262144 | tf_op jit(solution)/shard_map/all_to_all | solution.py:328
  73.6 2.3 %shard_map.74 = (f32[256,128]{1,0:T(8,128)S(1)}, f32[8,128]{1,0:T(8,128)S(1)}) custom-call(f32[256,128]{1,0:T(8,128)S(1)} %bitcast.39, s32[4,1024]{1,0:T(4,128)S(1)} %copy-done.2, f32[1,1024]{1,0:T(1,128)S(1)} %bitcast.49), custom_call_target="tpu_custom_call" | custom-call | tf_op jit(solution)/shard_map/pallas_call | solution.py:392
  75.8 11.4 %all_to_all.54 = f32[32,1,8,128]{3,2,1,0:T(8,128)S(1)} all-to-all(f32[32,1,8,128]{3,2,1,0:T(8,128)S(1)} %bitcast.48), channel_id=1, replica_groups=mesh['y'=4,'x'=4,'core'=2,'th'=4,'tl'=4] {'x','core','y'}, dimensions={0} | all-to-all | bytes 262144 | tf_op jit(solution)/shard_map/all_to_all | solution.py:328
  87.3 18.4 %all_to_all.55 = f32[16,2,8,128]{3,2,1,0:T(8,128)S(1)} all-to-all(f32[16,2,8,128]{3,2,1,0:T(8,128)S(1)} %bitcast.47), channel_id=1, replica_groups=mesh['y'=4,'x'=4,'core'=2,'th'=4,'tl'=4] {'th','tl'}, dimensions={0} | all-to-all | bytes 262144 | tf_op jit(solution)/shard_map/all_to_all | solution.py:328
  105.6 0.9 shard_map.76
  106.6 18.7 %all_to_all.56 = f32[16,2,8,128]{3,2,1,0:T(8,128)S(1)} all-to-all(f32[16,2,8,128]{3,2,1,0:T(8,128)S(1)} %bitcast.34), channel_id=1, replica_groups=mesh['y'=4,'x'=4,'core'=2,'th'=4,'tl'=4] {'th','tl'}, dimensions={0} | all-to-all | bytes 262144 | tf_op jit(solution)/shard_map/all_to_all | solution.py:328
  125.3 0.1 shard_map.77
  125.4 10.5 %all_to_all.57 = f32[32,1,8,128]{3,2,1,0:T(8,128)S(1)} all-to-all(f32[32,1,8,128]{3,2,1,0:T(8,128)S(1)} %bitcast.41), channel_id=1, replica_groups=mesh['y'=4,'x'=4,'core'=2,'th'=4,'tl'=4] {'x','core','y'}, dimensions={0} | all-to-all | bytes 262144 | tf_op jit(solution)/shard_map/all_to_all | solution.py:328
  135.9 2.3 %shard_map.78 = f32[288,128]{1,0:T(8,128)S(1)} custom-call(f32[256,128]{1,0:T(8,128)S(1)} %bitcast.38, s32[4,1024]{1,0:T(4,128)S(1)} %copy-done.2, f32[1,1024]{1,0:T(1,128)S(1)} %bitcast.50, f32[8,128]{1,0:T(8,128)S(1)} %get-tuple-element.5.refs_0_), custom_call_target="tpu_custom_call" | custom-call | tf_op jit(solution)/shard_map/pallas_call | solution.py:392
  138.2 11.6 %all_to_all.58 = f32[32,9,1,128]{3,2,1,0:T(1,128)S(1)} all-to-all(f32[32,9,1,128]{3,2,1,0:T(1,128)S(1)} %bitcast.29), channel_id=1, replica_groups=mesh['y'=4,'x'=4,'core'=2,'th'=4,'tl'=4] {'x','core','y'}, dimensions={0} | all-to-all | bytes 294912 | tf_op jit(solution)/shard_map/all_to_all | solution.py:328
  149.8 18.8 %all_to_all.59 = f32[16,17,1,128]{3,2,1,0:T(1,128)S(1)} all-to-all(f32[16,17,1,128]{3,2,1,0:T(1,128)S(1)} %bitcast.32), channel_id=1, replica_groups=mesh['y'=4,'x'=4,'core'=2,'th'=4,'tl'=4] {'th','tl'}, dimensions={0} | all-to-all | bytes 278528 | tf_op jit(solution)/shard_map/all_to_all | solution.py:328
  168.5 0.8 shard_map.80
  (9 shorter events, 0.1 us)
Async XLA Ops:
  0.6 0.7 copy-start.4
  0.6 0.9 copy-start.1
  0.7 39.7 %copy-start = (bf16[4,2,256,256]{3,2,1,0:T(8,128)(2,1)S(1)}, bf16[4,2,256,256]{3,2,1,0:T(8,128)(2,1)}, u32[]{:S(2)}) copy-start(bf16[4,2,256,256]{3,2,1,0:T(8,128)(2,1)} %constant.9.clone.waves_ref) | copy-start | bytes 3145732
  59.5 14.1 %copy-start.2 = (s32[4,1024]{1,0:T(4,128)S(1)}, s32[4,1024]{1,0:T(4,128)}, u32[]{:S(2)}) copy-start(s32[4,1024]{1,0:T(4,128)} %quartets_ref.3) | copy-start | bytes 49156
  59.5 14.1 %copy-start.3 = (f32[1024]{0:T(1024)S(1)}, f32[1024]{0:T(1024)}, u32[]{:S(2)}) copy-start(f32[1024]{0:T(1024)} %param.8) | copy-start | bytes 12292

commit v8 on v6

--- a/solution.py
+++ b/solution.py
@@ -13,6 +13,7 @@
 
 STEPS = 2
 LANES = 128
+BACKWARD = (0, 2, 1, 3)
 TIME = 65536
 QUARTER = TIME // 4
 TILE = 256
@@ -167,7 +168,7 @@
             pair = turned_back(y[f], *twist(f * (place + v2 * 4096))) if f else y[f]
             for ri in range(2):
                 for v0 in range(2):
-                    first = f * 64 + ri * 8 + v2 * 2 + v0
+                    first = BACKWARD[f] * 64 + ri * 8 + v2 * 2 + v0
                     out_ref[pl.ds(first, 4, stride=16), :] = pair[ri][v0 * 4 : v0 * 4 + 4]
 
 
@@ -206,10 +207,11 @@
                 out_ref[pl.ds(a * 64 + low * 2 + ri, 8, stride=8), :] = pair[ri]
 
 
-def spectral_kernel(x_ref, rotor_ref, small_ref, waves_ref, out_ref):
+def spectral_kernel(order, x_ref, rotor_ref, small_ref, waves_ref, out_ref):
     rotor = (rotor_ref[0], rotor_ref[1])
     small = (small_ref[0], small_ref[1])
-    y = from_left(waves_ref, 0, x_ref[...])
+    x = jnp.concatenate([x_ref[64 * k : 64 * k + 64, :] for k in order], axis=0)
+    y = from_left(waves_ref, 0, x)
     re, im = turned_back((y[:LANES], y[LANES:]), *small)
     y = from_right(jnp.concatenate([re, im], axis=1), waves_ref, 1)
     re, im = turned((y[:, :LANES], y[:, LANES:]), *rotor)
@@ -328,9 +330,9 @@
 
 def shards(field, beta, quartets, intersections):
     waves = jnp.asarray(host_waves())
-    th, tl = (lax.axis_index(a).astype(jnp.int32)[None] for a in ("th", "tl"))
+    th, tl = (lax.axis_index(a).astype(jnp.int32)[None] for a in ("th", ("t1", "t0")))
     weights = intersections.reshape(1, -1)
-    along, across = (("th", "tl"), "mode")
+    along, across = (("th", "t1", "t0"), "mode")
     vmem = pl.BlockSpec(memory_space=pltpu.VMEM)
     smem = pl.BlockSpec(memory_space=pltpu.SMEM)
     limit = pltpu.CompilerParams(vmem_limit_bytes=16 * 1024 * 1024)
@@ -344,9 +346,9 @@
             compiler_params=limit,
         )(*numbers, state)
 
-    def spectral(state):
+    def spectral(state, order):
         return pl.pallas_call(
-            spectral_kernel,
+            functools.partial(spectral_kernel, order),
             out_shape=rows_of(256),
             in_specs=[vmem] * 4,
             out_specs=vmem,
@@ -379,11 +381,11 @@
     )(field, rotor)
     state = exchange(state, along, 16)
     state = placed(first_radix_kernel, state, tl)
-    state = exchange(state, "tl", 4)
+    state = exchange(state, ("t0", "t1"), 4)
     norms = []
     for step in range(STEPS):
         last = step == STEPS - 1
-        state = spectral(state)
+        state = spectral(state, range(4) if step else BACKWARD)
         state = exchange(state, along, 16)
         state = placed(back_kernel, state, th, tl)
         state = exchange(state, across, 32)
@@ -424,8 +426,8 @@
 
 
 def solution(mesh):
-    finer = Mesh(mesh.devices.reshape(-1, 4, 4), ("mode", "th", "tl"))
-    times = ("th", "tl")
+    finer = Mesh(mesh.devices.reshape(-1, 4, 2, 2), ("mode", "th", "t1", "t0"))
+    times = ("th", "t1", "t0")
     return jax.shard_map(
         shards,
         mesh=finer,

time: 170 us -> 170 us (level)
  no operation moved by 1% of the time
where the time goes in v8:
time: 170 us
  blocking collectives  160 us (94%)
  Pallas kernels  7.9 us (5%)
    all_to_all x10, blocking collectives, exchange(): return lax.all_to_all(tiles, axes, 0, 0, tiled=True).reshape(array.shape)  160 us
    pallas_call x2, Pallas kernels, shards(): pl.pallas_call(functools.partial(kerr_kernel, last), out_shape=rows_of(28...  4.63 us

profile of v8, /device:TPU:32, one launch (start us, length us, event | category | flops | bytes accessed | tf_op | source)
XLA Modules:
  0.0 169.7 jit_solution(24483886924480659)
XLA Ops:
  0.7 0.1 shard_map.68.after_ref.small_ref
  0.8 0.0 copy-start
  0.8 0.5 copy-done.4
  1.3 0.2 shard_map.69.after_ref.rotor_ref
  1.5 0.0 copy-done.1
  1.6 0.1 shard_map.70
  1.6 29.2 %all_to_all.50 = f32[16,2,8,128]{3,2,1,0:T(8,128)S(1)} all-to-all(f32[16,2,8,128]{3,2,1,0:T(8,128)S(1)} %bitcast.37), channel_id=1, replica_groups=mesh['mode'=32,'th'=4,'t1'=2,'t0'=2] {'th','t1','t0'}, dimensions={0} | all-to-all | bytes 262144 | tf_op jit(solution)/shard_map/all_to_all | solution.py:328
  30.9 0.1 shard_map.71
  31.0 8.5 %all_to_all.51 = f32[4,8,8,128]{3,2,1,0:T(8,128)S(1)} all-to-all(f32[4,8,8,128]{3,2,1,0:T(8,128)S(1)} %bitcast.43), channel_id=1, replica_groups=mesh['mode'=32,'th'=4,'t1'=2,'t0'=2] {'t0','t1'}, dimensions={0} | all-to-all | bytes 262144 | tf_op jit(solution)/shard_map/all_to_all | solution.py:328
  39.5 0.9 shard_map.72
  40.4 18.5 %all_to_all.52 = f32[16,2,8,128]{3,2,1,0:T(8,128)S(1)} all-to-all(f32[16,2,8,128]{3,2,1,0:T(8,128)S(1)} %bitcast.36), channel_id=1, replica_groups=mesh['mode'=32,'th'=4,'t1'=2,'t0'=2] {'th','t1','t0'}, dimensions={0} | all-to-all | bytes 262144 | tf_op jit(solution)/shard_map/all_to_all | solution.py:328
  58.9 0.1 shard_map.73
  59.0 14.9 %all_to_all.53 = f32[32,1,8,128]{3,2,1,0:T(8,128)S(1)} all-to-all(f32[32,1,8,128]{3,2,1,0:T(8,128)S(1)} %bitcast.45), channel_id=1, replica_groups=mesh['mode'=32,'th'=4,'t1'=2,'t0'=2] {'mode'}, dimensions={0} | all-to-all | bytes 262144 | tf_op jit(solution)/shard_map/all_to_all | solution.py:328
  73.9 2.3 %shard_map.74 = (f32[256,128]{1,0:T(8,128)S(1)}, f32[8,128]{1,0:T(8,128)S(1)}) custom-call(f32[256,128]{1,0:T(8,128)S(1)} %bitcast.39, s32[4,1024]{1,0:T(4,128)S(1)} %copy-done.2, f32[1,1024]{1,0:T(1,128)S(1)} %bitcast.49), custom_call_target="tpu_custom_call" | custom-call | tf_op jit(solution)/shard_map/pallas_call | solution.py:392
  76.2 11.2 %all_to_all.54 = f32[32,1,8,128]{3,2,1,0:T(8,128)S(1)} all-to-all(f32[32,1,8,128]{3,2,1,0:T(8,128)S(1)} %bitcast.48), channel_id=1, replica_groups=mesh['mode'=32,'th'=4,'t1'=2,'t0'=2] {'mode'}, dimensions={0} | all-to-all | bytes 262144 | tf_op jit(solution)/shard_map/all_to_all | solution.py:328
  87.5 18.1 %all_to_all.55 = f32[16,2,8,128]{3,2,1,0:T(8,128)S(1)} all-to-all(f32[16,2,8,128]{3,2,1,0:T(8,128)S(1)} %bitcast.47), channel_id=1, replica_groups=mesh['mode'=32,'th'=4,'t1'=2,'t0'=2] {'th','t1','t0'}, dimensions={0} | all-to-all | bytes 262144 | tf_op jit(solution)/shard_map/all_to_all | solution.py:328
  105.6 0.9 shard_map.76
  106.6 19.1 %all_to_all.56 = f32[16,2,8,128]{3,2,1,0:T(8,128)S(1)} all-to-all(f32[16,2,8,128]{3,2,1,0:T(8,128)S(1)} %bitcast.34), channel_id=1, replica_groups=mesh['mode'=32,'th'=4,'t1'=2,'t0'=2] {'th','t1','t0'}, dimensions={0} | all-to-all | bytes 262144 | tf_op jit(solution)/shard_map/all_to_all | solution.py:328
  125.7 0.1 shard_map.77
  125.8 11.2 %all_to_all.57 = f32[32,1,8,128]{3,2,1,0:T(8,128)S(1)} all-to-all(f32[32,1,8,128]{3,2,1,0:T(8,128)S(1)} %bitcast.41), channel_id=1, replica_groups=mesh['mode'=32,'th'=4,'t1'=2,'t0'=2] {'mode'}, dimensions={0} | all-to-all | bytes 262144 | tf_op jit(solution)/shard_map/all_to_all | solution.py:328
  136.9 2.3 %shard_map.78 = f32[288,128]{1,0:T(8,128)S(1)} custom-call(f32[256,128]{1,0:T(8,128)S(1)} %bitcast.38, s32[4,1024]{1,0:T(4,128)S(1)} %copy-done.2, f32[1,1024]{1,0:T(1,128)S(1)} %bitcast.50, f32[8,128]{1,0:T(8,128)S(1)} %get-tuple-element.5.refs_0_), custom_call_target="tpu_custom_call" | custom-call | tf_op jit(solution)/shard_map/pallas_call | solution.py:392
  139.3 11.4 %all_to_all.58 = f32[32,9,1,128]{3,2,1,0:T(1,128)S(1)} all-to-all(f32[32,9,1,128]{3,2,1,0:T(1,128)S(1)} %bitcast.29), channel_id=1, replica_groups=mesh['mode'=32,'th'=4,'t1'=2,'t0'=2] {'mode'}, dimensions={0} | all-to-all | bytes 294912 | tf_op jit(solution)/shard_map/all_to_all | solution.py:328
  150.7 18.3 %all_to_all.59 = f32[16,17,1,128]{3,2,1,0:T(1,128)S(1)} all-to-all(f32[16,17,1,128]{3,2,1,0:T(1,128)S(1)} %bitcast.32), channel_id=1, replica_groups=mesh['mode'=32,'th'=4,'t1'=2,'t0'=2] {'th','t1','t0'}, dimensions={0} | all-to-all | bytes 278528 | tf_op jit(solution)/shard_map/all_to_all | solution.py:328
  169.0 0.8 shard_map.80
  (9 shorter events, 0.1 us)
Async XLA Ops:
  0.6 0.7 copy-start.4
  0.6 0.9 copy-start.1
  0.8 38.7 %copy-start = (bf16[4,2,256,256]{3,2,1,0:T(8,128)(2,1)S(1)}, bf16[4,2,256,256]{3,2,1,0:T(8,128)(2,1)}, u32[]{:S(2)}) copy-start(bf16[4,2,256,256]{3,2,1,0:T(8,128)(2,1)} %constant.15.clone.waves_ref) | copy-start | bytes 3145732
  59.0 14.9 %copy-start.2 = (s32[4,1024]{1,0:T(4,128)S(1)}, s32[4,1024]{1,0:T(4,128)}, u32[]{:S(2)}) copy-start(s32[4,1024]{1,0:T(4,128)} %quartets_ref.3) | copy-start | bytes 49156
  59.0 14.9 %copy-start.3 = (f32[1024]{0:T(1024)S(1)}, f32[1024]{0:T(1024)}, u32[]{:S(2)}) copy-start(f32[1024]{0:T(1024)} %param.8) | copy-start | bytes 12292

commit v9 on v8

--- a/solution.py
+++ b/solution.py
@@ -132,7 +132,8 @@
     for ri in range(2):
         for tile in range(32):
             zb, rest = (tile // 4 % 4, tile // 16 * 4 + tile % 4)
-            out_ref[pl.ds(zb * 16 + ri * 8 + rest, 4, stride=64), :] = field_ref[
+            at = BACKWARD[zb] * 16 + ri * 8 + rest
+            out_ref[pl.ds(at, 4, stride=64), :] = field_ref[
                 ri, :, tile * LANES : (tile + 1) * LANES
             ]
 
@@ -162,7 +163,7 @@
     row, lane = row_and_lane()
     place = (row // 4) * 2048 + (row % 4) * LANES + lane + zb_ref[0] * 512
     for v2 in range(4):
-        at = [a * 64 + v2 * 16 for a in range(4)]
+        at = [a * 64 + BACKWARD[v2] * 16 for a in range(4)]
         y = radix_ahead([(x_ref[b : b + 8, :], x_ref[b + 8 : b + 16, :]) for b in at])
         for f in range(4):
             pair = turned_back(y[f], *twist(f * (place + v2 * 4096))) if f else y[f]
@@ -293,11 +294,12 @@
     for source in range(1, 32):
         norms = norms + x_ref[source * 9 + 8 : source * 9 + 9, :]
     for target in range(16):
+        place = target // 4 * 4 + BACKWARD[target % 4]
         for half in range(2):
             source = target * 2 + half
-            at = target * 17 + half * 8
+            at = place * 17 + half * 8
             out_ref[at : at + 8, :] = x_ref[source * 9 : source * 9 + 8, :]
-        out_ref[target * 17 + 16 : target * 17 + 17, :] = norms
+        out_ref[place * 17 + 16 : place * 17 + 17, :] = norms
 
 
 def leave_kernel(x_ref, field_ref, errors_ref):
@@ -310,7 +312,7 @@
     errors_ref[1:2, :] = ratio[:, 8:12]
     for source in range(16):
         for half in range(2):
-            tile = half * 16 + source
+            tile = half * 16 + source // 4 * 4 + BACKWARD[source % 4]
             for ri in range(2):
                 field_ref[ri, :, tile * LANES : (tile + 1) * LANES] = x_ref[
                     pl.ds(source * 17 + half * 8 + ri, 4, stride=2), :
@@ -379,7 +381,7 @@
         out_specs=vmem,
         compiler_params=limit,
     )(field, rotor)
-    state = exchange(state, along, 16)
+    state = exchange(state, ("th", "t0", "t1"), 16)
     state = placed(first_radix_kernel, state, tl)
     state = exchange(state, ("t0", "t1"), 4)
     norms = []
@@ -412,7 +414,7 @@
         out_specs=vmem,
         compiler_params=limit,
     )(state)
-    state = exchange(state, along, 16)
+    state = exchange(state, ("th", "t0", "t1"), 16)
     return pl.pallas_call(
         leave_kernel,
         out_shape=(

time: 170 us -> 170 us (level)
  the two profiles are of different devices: /device:TPU:32 before, /device:TPU:2 now
where the time goes in v9:
time: 170 us; the launch traced here: 169 us
  blocking collectives  160 us (94%)
  Pallas kernels  7.89 us (5%)
    all_to_all x10, blocking collectives, exchange(): return lax.all_to_all(tiles, axes, 0, 0, tiled=True).reshape(array.shape)  160 us
    pallas_call x2, Pallas kernels, shards(): pl.pallas_call(functools.partial(kerr_kernel, last), out_shape=rows_of(28...  4.62 us

profile of v9, /device:TPU:2, one launch (start us, length us, event | category | flops | bytes accessed | tf_op | source)
XLA Modules:
  0.0 169.3 jit_solution(6780446466787529995)
XLA Ops:
  0.7 0.1 shard_map.68.after_ref.small_ref
  0.8 0.0 copy-start
  0.8 0.5 copy-done.4
  1.3 0.2 shard_map.69.after_ref.rotor_ref
  1.5 0.0 copy-done.1
  1.6 0.1 shard_map.70
  1.6 29.9 %all_to_all.50 = f32[16,2,8,128]{3,2,1,0:T(8,128)S(1)} all-to-all(f32[16,2,8,128]{3,2,1,0:T(8,128)S(1)} %bitcast.37), channel_id=1, replica_groups=mesh['mode'=32,'th'=4,'t1'=2,'t0'=2] {'th','t0','t1'}, dimensions={0} | all-to-all | bytes 262144 | tf_op jit(solution)/shard_map/all_to_all | solution.py:330
  31.5 0.1 shard_map.71
  31.6 8.9 %all_to_all.51 = f32[4,8,8,128]{3,2,1,0:T(8,128)S(1)} all-to-all(f32[4,8,8,128]{3,2,1,0:T(8,128)S(1)} %bitcast.43), channel_id=1, replica_groups=mesh['mode'=32,'th'=4,'t1'=2,'t0'=2] {'t0','t1'}, dimensions={0} | all-to-all | bytes 262144 | tf_op jit(solution)/shard_map/all_to_all | solution.py:330
  40.5 0.9 shard_map.72
  41.5 18.0 %all_to_all.52 = f32[16,2,8,128]{3,2,1,0:T(8,128)S(1)} all-to-all(f32[16,2,8,128]{3,2,1,0:T(8,128)S(1)} %bitcast.36), channel_id=1, replica_groups=mesh['mode'=32,'th'=4,'t1'=2,'t0'=2] {'th','t1','t0'}, dimensions={0} | all-to-all | bytes 262144 | tf_op jit(solution)/shard_map/all_to_all | solution.py:330
  59.4 0.1 shard_map.73
  59.5 14.0 %all_to_all.53 = f32[32,1,8,128]{3,2,1,0:T(8,128)S(1)} all-to-all(f32[32,1,8,128]{3,2,1,0:T(8,128)S(1)} %bitcast.45), channel_id=1, replica_groups=mesh['mode'=32,'th'=4,'t1'=2,'t0'=2] {'mode'}, dimensions={0} | all-to-all | bytes 262144 | tf_op jit(solution)/shard_map/all_to_all | solution.py:330
  73.5 2.3 %shard_map.74 = (f32[256,128]{1,0:T(8,128)S(1)}, f32[8,128]{1,0:T(8,128)S(1)}) custom-call(f32[256,128]{1,0:T(8,128)S(1)} %bitcast.39, s32[4,1024]{1,0:T(4,128)S(1)} %copy-done.2, f32[1,1024]{1,0:T(1,128)S(1)} %bitcast.49), custom_call_target="tpu_custom_call" | custom-call | tf_op jit(solution)/shard_map/pallas_call | solution.py:394
  75.8 11.3 %all_to_all.54 = f32[32,1,8,128]{3,2,1,0:T(8,128)S(1)} all-to-all(f32[32,1,8,128]{3,2,1,0:T(8,128)S(1)} %bitcast.48), channel_id=1, replica_groups=mesh['mode'=32,'th'=4,'t1'=2,'t0'=2] {'mode'}, dimensions={0} | all-to-all | bytes 262144 | tf_op jit(solution)/shard_map/all_to_all | solution.py:330
  87.2 18.4 %all_to_all.55 = f32[16,2,8,128]{3,2,1,0:T(8,128)S(1)} all-to-all(f32[16,2,8,128]{3,2,1,0:T(8,128)S(1)} %bitcast.47), channel_id=1, replica_groups=mesh['mode'=32,'th'=4,'t1'=2,'t0'=2] {'th','t1','t0'}, dimensions={0} | all-to-all | bytes 262144 | tf_op jit(solution)/shard_map/all_to_all | solution.py:330
  105.6 0.9 shard_map.76
  106.5 18.7 %all_to_all.56 = f32[16,2,8,128]{3,2,1,0:T(8,128)S(1)} all-to-all(f32[16,2,8,128]{3,2,1,0:T(8,128)S(1)} %bitcast.34), channel_id=1, replica_groups=mesh['mode'=32,'th'=4,'t1'=2,'t0'=2] {'th','t1','t0'}, dimensions={0} | all-to-all | bytes 262144 | tf_op jit(solution)/shard_map/all_to_all | solution.py:330
  125.3 0.1 shard_map.77
  125.3 11.1 %all_to_all.57 = f32[32,1,8,128]{3,2,1,0:T(8,128)S(1)} all-to-all(f32[32,1,8,128]{3,2,1,0:T(8,128)S(1)} %bitcast.41), channel_id=1, replica_groups=mesh['mode'=32,'th'=4,'t1'=2,'t0'=2] {'mode'}, dimensions={0} | all-to-all | bytes 262144 | tf_op jit(solution)/shard_map/all_to_all | solution.py:330
  136.4 2.3 %shard_map.78 = f32[288,128]{1,0:T(8,128)S(1)} custom-call(f32[256,128]{1,0:T(8,128)S(1)} %bitcast.38, s32[4,1024]{1,0:T(4,128)S(1)} %copy-done.2, f32[1,1024]{1,0:T(1,128)S(1)} %bitcast.50, f32[8,128]{1,0:T(8,128)S(1)} %get-tuple-element.5.refs_0_), custom_call_target="tpu_custom_call" | custom-call | tf_op jit(solution)/shard_map/pallas_call | solution.py:394
  138.7 11.4 %all_to_all.58 = f32[32,9,1,128]{3,2,1,0:T(1,128)S(1)} all-to-all(f32[32,9,1,128]{3,2,1,0:T(1,128)S(1)} %bitcast.29), channel_id=1, replica_groups=mesh['mode'=32,'th'=4,'t1'=2,'t0'=2] {'mode'}, dimensions={0} | all-to-all | bytes 294912 | tf_op jit(solution)/shard_map/all_to_all | solution.py:330
  150.2 18.4 %all_to_all.59 = f32[16,17,1,128]{3,2,1,0:T(1,128)S(1)} all-to-all(f32[16,17,1,128]{3,2,1,0:T(1,128)S(1)} %bitcast.32), channel_id=1, replica_groups=mesh['mode'=32,'th'=4,'t1'=2,'t0'=2] {'th','t0','t1'}, dimensions={0} | all-to-all | bytes 278528 | tf_op jit(solution)/shard_map/all_to_all | solution.py:330
  168.5 0.8 shard_map.80
  (9 shorter events, 0.1 us)
Async XLA Ops:
  0.6 0.7 copy-start.4
  0.6 0.9 copy-start.1
  0.8 39.8 %copy-start = (bf16[4,2,256,256]{3,2,1,0:T(8,128)(2,1)S(1)}, bf16[4,2,256,256]{3,2,1,0:T(8,128)(2,1)}, u32[]{:S(2)}) copy-start(bf16[4,2,256,256]{3,2,1,0:T(8,128)(2,1)} %constant.15.clone.waves_ref) | copy-start | bytes 3145732
  59.5 14.1 %copy-start.2 = (s32[4,1024]{1,0:T(4,128)S(1)}, s32[4,1024]{1,0:T(4,128)}, u32[]{:S(2)}) copy-start(s32[4,1024]{1,0:T(4,128)} %quartets_ref.3) | copy-start | bytes 49156
  59.5 14.1 %copy-start.3 = (f32[1024]{0:T(1024)S(1)}, f32[1024]{0:T(1024)}, u32[]{:S(2)}) copy-start(f32[1024]{0:T(1024)} %param.8) | copy-start | bytes 12292

commit v10 on v8

--- a/solution.py
+++ b/solution.py
@@ -323,7 +323,7 @@
 
 def exchange(array, axes, peers):
     rows = array.shape[0] // peers
-    tile = 8 if rows % 8 == 0 else 1
+    tile = 1
     tiles = array.reshape(peers, rows // tile, tile, LANES)
     return lax.all_to_all(tiles, axes, 0, 0, tiled=True).reshape(array.shape)
 

time: 170 us -> 170 us (level)
  no operation moved by 1% of the time
where the time goes in v10:
time: 170 us
  blocking collectives  160 us (94%)
  Pallas kernels  7.9 us (5%)
    all_to_all x10, blocking collectives, exchange(): return lax.all_to_all(tiles, axes, 0, 0, tiled=True).reshape(array.shape)  160 us
    pallas_call x2, Pallas kernels, shards(): pl.pallas_call(functools.partial(kerr_kernel, last), out_shape=rows_of(28...  4.63 us

profile of v10, /device:TPU:32, one launch (start us, length us, event | category | flops | bytes accessed | tf_op | source)
XLA Modules:
  0.0 169.7 jit_solution(24483886924480659)
XLA Ops:
  0.7 0.1 shard_map.68.after_ref.small_ref
  0.8 0.0 copy-start
  0.8 0.5 copy-done.4
  1.3 0.2 shard_map.69.after_ref.rotor_ref
  1.5 0.0 copy-done.1
  1.6 0.1 shard_map.70
  1.6 29.2 %all_to_all.50 = f32[16,16,1,128]{3,1,2,0:T(8,128)S(1)} all-to-all(f32[16,16,1,128]{3,1,2,0:T(8,128)S(1)} %bitcast.47), channel_id=1, replica_groups=mesh['mode'=32,'th'=4,'t1'=2,'t0'=2] {'th','t1','t0'}, dimensions={0} | all-to-all | bytes 262144 | tf_op jit(solution)/shard_map/all_to_all | solution.py:328
  30.9 0.1 shard_map.71
  31.0 8.5 %all_to_all.51 = f32[4,64,1,128]{3,1,2,0:T(8,128)S(1)} all-to-all(f32[4,64,1,128]{3,1,2,0:T(8,128)S(1)} %bitcast.53), channel_id=1, replica_groups=mesh['mode'=32,'th'=4,'t1'=2,'t0'=2] {'t0','t1'}, dimensions={0} | all-to-all | bytes 262144 | tf_op jit(solution)/shard_map/all_to_all | solution.py:328
  39.5 0.9 shard_map.72
  40.4 18.5 %all_to_all.52 = f32[16,16,1,128]{3,1,2,0:T(8,128)S(1)} all-to-all(f32[16,16,1,128]{3,1,2,0:T(8,128)S(1)} %bitcast.46), channel_id=1, replica_groups=mesh['mode'=32,'th'=4,'t1'=2,'t0'=2] {'th','t1','t0'}, dimensions={0} | all-to-all | bytes 262144 | tf_op jit(solution)/shard_map/all_to_all | solution.py:328
  58.9 0.1 shard_map.73
  59.0 14.9 %all_to_all.53 = f32[32,8,1,128]{3,1,2,0:T(8,128)S(1)} all-to-all(f32[32,8,1,128]{3,1,2,0:T(8,128)S(1)} %bitcast.55), channel_id=1, replica_groups=mesh['mode'=32,'th'=4,'t1'=2,'t0'=2] {'mode'}, dimensions={0} | all-to-all | bytes 262144 | tf_op jit(solution)/shard_map/all_to_all | solution.py:328
  73.9 2.3 %shard_map.74 = (f32[256,128]{1,0:T(8,128)S(1)}, f32[8,128]{1,0:T(8,128)S(1)}) custom-call(f32[256,128]{1,0:T(8,128)S(1)} %bitcast.49, s32[4,1024]{1,0:T(4,128)S(1)} %copy-done.2, f32[1,1024]{1,0:T(1,128)S(1)} %bitcast.59), custom_call_target="tpu_custom_call" | custom-call | tf_op jit(solution)/shard_map/pallas_call | solution.py:392
  76.2 11.2 %all_to_all.54 = f32[32,8,1,128]{3,1,2,0:T(8,128)S(1)} all-to-all(f32[32,8,1,128]{3,1,2,0:T(8,128)S(1)} %bitcast.58), channel_id=1, replica_groups=mesh['mode'=32,'th'=4,'t1'=2,'t0'=2] {'mode'}, dimensions={0} | all-to-all | bytes 262144 | tf_op jit(solution)/shard_map/all_to_all | solution.py:328
  87.5 18.1 %all_to_all.55 = f32[16,16,1,128]{3,1,2,0:T(8,128)S(1)} all-to-all(f32[16,16,1,128]{3,1,2,0:T(8,128)S(1)} %bitcast.57), channel_id=1, replica_groups=mesh['mode'=32,'th'=4,'t1'=2,'t0'=2] {'th','t1','t0'}, dimensions={0} | all-to-all | bytes 262144 | tf_op jit(solution)/shard_map/all_to_all | solution.py:328
  105.6 0.9 shard_map.76
  106.6 19.1 %all_to_all.56 = f32[16,16,1,128]{3,1,2,0:T(8,128)S(1)} all-to-all(f32[16,16,1,128]{3,1,2,0:T(8,128)S(1)} %bitcast.44), channel_id=1, replica_groups=mesh['mode'=32,'th'=4,'t1'=2,'t0'=2] {'th','t1','t0'}, dimensions={0} | all-to-all | bytes 262144 | tf_op jit(solution)/shard_map/all_to_all | solution.py:328
  125.7 0.1 shard_map.77
  125.8 11.2 %all_to_all.57 = f32[32,8,1,128]{3,1,2,0:T(8,128)S(1)} all-to-all(f32[32,8,1,128]{3,1,2,0:T(8,128)S(1)} %bitcast.51), channel_id=1, replica_groups=mesh['mode'=32,'th'=4,'t1'=2,'t0'=2] {'mode'}, dimensions={0} | all-to-all | bytes 262144 | tf_op jit(solution)/shard_map/all_to_all | solution.py:328
  136.9 2.3 %shard_map.78 = f32[288,128]{1,0:T(8,128)S(1)} custom-call(f32[256,128]{1,0:T(8,128)S(1)} %bitcast.48, s32[4,1024]{1,0:T(4,128)S(1)} %copy-done.2, f32[1,1024]{1,0:T(1,128)S(1)} %bitcast.60, f32[8,128]{1,0:T(8,128)S(1)} %get-tuple-element.5.refs_0_), custom_call_target="tpu_custom_call" | custom-call | tf_op jit(solution)/shard_map/pallas_call | solution.py:392
  139.3 11.4 %all_to_all.58 = f32[32,9,1,128]{3,2,1,0:T(1,128)S(1)} all-to-all(f32[32,9,1,128]{3,2,1,0:T(1,128)S(1)} %bitcast.39), channel_id=1, replica_groups=mesh['mode'=32,'th'=4,'t1'=2,'t0'=2] {'mode'}, dimensions={0} | all-to-all | bytes 294912 | tf_op jit(solution)/shard_map/all_to_all | solution.py:328
  150.7 18.3 %all_to_all.59 = f32[16,17,1,128]{3,2,1,0:T(1,128)S(1)} all-to-all(f32[16,17,1,128]{3,2,1,0:T(1,128)S(1)} %bitcast.42), channel_id=1, replica_groups=mesh['mode'=32,'th'=4,'t1'=2,'t0'=2] {'th','t1','t0'}, dimensions={0} | all-to-all | bytes 278528 | tf_op jit(solution)/shard_map/all_to_all | solution.py:328
  169.0 0.8 shard_map.80
  (9 shorter events, 0.1 us)
Async XLA Ops:
  0.6 0.7 copy-start.4
  0.6 0.9 copy-start.1
  0.8 38.7 %copy-start = (bf16[4,2,256,256]{3,2,1,0:T(8,128)(2,1)S(1)}, bf16[4,2,256,256]{3,2,1,0:T(8,128)(2,1)}, u32[]{:S(2)}) copy-start(bf16[4,2,256,256]{3,2,1,0:T(8,128)(2,1)} %constant.15.clone.waves_ref) | copy-start | bytes 3145732
  59.0 14.9 %copy-start.2 = (s32[4,1024]{1,0:T(4,128)S(1)}, s32[4,1024]{1,0:T(4,128)}, u32[]{:S(2)}) copy-start(s32[4,1024]{1,0:T(4,128)} %quartets_ref.3) | copy-start | bytes 49156
  59.0 14.9 %copy-start.3 = (f32[1024]{0:T(1024)S(1)}, f32[1024]{0:T(1024)}, u32[]{:S(2)}) copy-start(f32[1024]{0:T(1024)} %param.8) | copy-start | bytes 12292
